TPU v7x, 32 devices: a whole 2x2x4 slice. The times are simulated.
32 devices in a mesh: blocks: 32 (over z, y, x, core).
Axes of the slice: x: 2, y: 2, z: 4, core: 2. Of those that a mesh axis runs over, the one named last changes fastest.
Arguments:
- old_pdfs: float32 [64, 19, 32768], P('blocks'), may hold values from 0 to 0.5
- old_slot: int32 [32], replicated, may hold values from 0 to 63, as said below
- neighbours: int32 [32, 18], P('blocks'), may hold values from -1 to 31, as said below
- cell_flags: int32 [32, 32768], P('blocks'), may hold values from 0 to 3, as said below
Outputs:
- new_pdfs: float32 [32, 19, 32768], P('blocks')
Inputs may be any that keep to these rules, and one draw needn't show every extreme that they name: `old_slot`: distinct slots; slot s lies on device s // 2 before migration; in every draw some device has all 2 of its slots in use. `neighbours`: the blocks form 8 layers of 2 x 2 blocks along a vessel, blocks 4 * l to 4 * l + 3 making layer l; column d names the block at block offset c_(d+1), or -1 where there is none; the relation is mutual. `cell_flags`: 0 fluid, 1 wall, 2 inlet, 3 outlet; the cells on the outermost layer of every block are fluid.
All inputs are finite; a program needn't handle non-finite values.
Results may differ from a plain program's by a relative error of at most 0.0003.
Values sent between devices are 32-bit elements; how exact they have to be, the bound alone decides.
A program may use at most 192 MiB of HBM per device.

v0:
```python
import jax
import jax.numpy as jnp
import numpy as np
from jax import lax
from jax.sharding import PartitionSpec as P

EDGE = 32
STEPS = 2


VELOCITY = (
    (0, 0, 0),
    (1, 0, 0),
    (-1, 0, 0),
    (0, 1, 0),
    (0, -1, 0),
    (0, 0, 1),
    (0, 0, -1),
    (1, 1, 0),
    (-1, -1, 0),
    (1, -1, 0),
    (-1, 1, 0),
    (1, 0, 1),
    (-1, 0, -1),
    (1, 0, -1),
    (-1, 0, 1),
    (0, 1, 1),
    (0, -1, -1),
    (0, 1, -1),
    (0, -1, 1),
)
WEIGHT_LIST = (1.0 / 3.0,) + (1.0 / 18.0,) * 6 + (1.0 / 36.0,) * 12
RELAXATION = (
    0.0,
    0.0,
    0.0,
    0.0,
    1.19,
    1.4,
    1.2,
    1.2,
    1.2,
    1.6,
    1.6,
    1.6,
    1.6,
    1.6,
    1.4,
    1.4,
    1.98,
    1.98,
    1.98,
)
INLET_SPEED = (0.0, 0.0, 0.05)


def from_behind(shard, axis, by):
    peers = lax.axis_size(axis)
    pairs = [(i, i + by) for i in range(peers) if 0 <= i + by < peers]
    return lax.ppermute(shard, axis, pairs)


def collision_table():
    lattice = np.array(VELOCITY) * 1.0
    along_x, along_y, along_z = (lattice[:, 0], lattice[:, 1], lattice[:, 2])
    squared = along_x * along_x + along_y * along_y + along_z * along_z
    monomials = [
        np.ones(19),
        along_x,
        along_y,
        along_z,
        squared,
        squared * squared,
        squared * along_x,
        squared * along_y,
        squared * along_z,
        3.0 * along_x * along_x - squared,
        along_y * along_y - along_z * along_z,
        along_x * along_y,
        along_y * along_z,
        along_x * along_z,
        squared * (3.0 * along_x * along_x - squared),
        squared * (along_y * along_y - along_z * along_z),
        (along_y * along_y - along_z * along_z) * along_x,
        (along_z * along_z - along_x * along_x) * along_y,
        (along_x * along_x - along_y * along_y) * along_z,
    ]
    orthonormal = []
    for vector in monomials:
        for earlier in orthonormal:
            vector = vector - np.dot(vector, earlier) * earlier
        orthonormal.append(vector / np.sqrt(np.dot(vector, vector)))
    stacked = np.stack(orthonormal)
    return stacked.T * np.array(RELAXATION) @ stacked


def opposite(index_value):
    if index_value == 0:
        return 0
    return index_value + 1 if index_value % 2 == 1 else index_value - 1


def ghost_region(offset, edge_size):
    return tuple(
        (
            (
                slice(0, 1)
                if component < 0
                else (
                    slice(edge_size + 1, edge_size + 2)
                    if component > 0
                    else slice(1, edge_size + 1)
                )
            )
            for component in offset
        )
    )


def outer_layer(offset, edge_size):
    return tuple(
        (
            (
                slice(edge_size - 1, edge_size)
                if component > 0
                else slice(0, 1) if component < 0 else slice(0, edge_size)
            )
            for component in offset
        )
    )


def channel_list(direction_code):
    offset = VELOCITY[direction_code + 1]
    if direction_code >= 6:
        return [direction_code + 1]
    axis_index = [component != 0 for component in offset].index(True)
    return [
        index_value
        for index_value in range(1, 19)
        if VELOCITY[index_value][axis_index] == offset[axis_index]
    ]


def collide(values, collision):
    lattice = jnp.asarray(VELOCITY, jnp.float32).T
    weights = jnp.asarray(WEIGHT_LIST, jnp.float32)[None, :, None]
    density = jnp.sum(values, axis=1, keepdims=True)
    momentum = jnp.einsum("ki,bin->bkn", lattice, values, precision=lax.Precision.HIGHEST)
    projected = jnp.einsum("ki,bkn->bin", lattice, momentum, precision=lax.Precision.HIGHEST)
    speed_square = jnp.sum(momentum * momentum, axis=1, keepdims=True)
    balance = weights * (
        density + 3.0 * projected + 4.5 * projected * projected - 1.5 * speed_square
    )
    return values - jnp.einsum(
        "pq,bqn->bpn", collision, values - balance, precision=lax.Precision.HIGHEST
    )


def propagate(padded, source_flags, collided_cells, block_flags):
    edge_size = block_flags.shape[-1]
    momentum = []
    for axis_index in range(3):
        running_sum = jnp.zeros_like(collided_cells[:, 0])
        for index_value in range(19):
            component = VELOCITY[index_value][axis_index]
            if component != 0:
                running_sum = running_sum + component * collided_cells[:, index_value]
        momentum.append(running_sum)
    speed_square = momentum[0] * momentum[0] + momentum[1] * momentum[1] + momentum[2] * momentum[2]
    inlet_square = sum((component * component for component in INLET_SPEED))
    results = []
    for index_value in range(19):
        offset = VELOCITY[index_value]
        weight = WEIGHT_LIST[index_value]
        window_slice = tuple(
            (slice(1 - component, 1 - component + edge_size) for component in offset)
        )
        pulled = padded[(slice(None), index_value) + window_slice]
        source_kind = source_flags[(slice(None),) + window_slice]
        bounce = collided_cells[:, opposite(index_value)]
        inlet_along = sum(
            (component * inlet_part for component, inlet_part in zip(offset, INLET_SPEED))
        )
        inlet_value = weight * (
            1.0 + 3.0 * inlet_along + 4.5 * inlet_along * inlet_along - 1.5 * inlet_square
        )
        outlet_along = offset[0] * momentum[0] + offset[1] * momentum[1] + offset[2] * momentum[2]
        outlet_value = weight * (
            1.0 + 3.0 * outlet_along + 4.5 * outlet_along * outlet_along - 1.5 * speed_square
        )
        new_value = jnp.where(
            source_kind == 0,
            pulled,
            jnp.where(
                source_kind == 1, bounce, jnp.where(source_kind == 2, inlet_value, outlet_value)
            ),
        )
        results.append(jnp.where(block_flags == 0, new_value, 0.0))
    return jnp.stack(results, axis=1)


def per_device(old_pdfs, old_slot, neighbours, cell_flags):
    collision = jnp.asarray(collision_table(), jnp.float32)
    blocks_here = neighbours.shape[0]
    cells_block = cell_flags.shape[1]
    edge_size = EDGE
    face_size = edge_size * edge_size
    spread = lax.all_to_all(old_pdfs, "blocks", split_axis=2, concat_axis=0, tiled=True)
    ordered = jnp.take(spread, old_slot, axis=0)
    arrived = lax.all_to_all(ordered, "blocks", split_axis=0, concat_axis=2, tiled=True)
    pdf_state = arrived.reshape(blocks_here, 19, edge_size, edge_size, edge_size)
    block_flags = cell_flags.reshape(blocks_here, edge_size, edge_size, edge_size)
    present = neighbours >= 0
    reach_devices = max(1, 7 // blocks_here)
    window_count = 2 * reach_devices + 1
    window_size = window_count * blocks_here
    my_index = lax.axis_index("blocks")
    first_block = (my_index - reach_devices) * blocks_here
    window_rows = jnp.clip(neighbours - first_block, 0, window_size - 1)
    face_index = window_rows[:, :6] * 6 + np.array(
        [code_value ^ 1 for code_value in range(6)], np.int32
    )
    edge_index = window_rows[:, 6:] * 12 + np.array(
        [(code_value ^ 1) - 6 for code_value in range(6, 18)], np.int32
    )
    for step_index in range(STEPS):
        collided_cells = collide(
            pdf_state.reshape(blocks_here, 19, cells_block), collision
        ).reshape(blocks_here, 19, edge_size, edge_size, edge_size)
        face_list = []
        edge_list = []
        for direction_code in range(18):
            layer_cells = (slice(None), slice(None)) + outer_layer(
                VELOCITY[direction_code + 1], edge_size
            )
            picked = collided_cells[:, np.array(channel_list(direction_code))][layer_cells]
            if direction_code < 6:
                face_list.append(picked.reshape(blocks_here, picked.shape[1], face_size))
            else:
                edge_list.append(picked.reshape(blocks_here, picked.shape[1], edge_size))
        face_messages = jnp.stack(face_list, axis=1)
        edge_messages = jnp.concatenate(edge_list, axis=2)
        edge_messages = edge_messages.reshape(blocks_here, 12 * edge_size)
        face_parts = []
        edge_parts = []
        for distance in range(-reach_devices, reach_devices + 1):
            if distance == 0:
                face_parts.append(face_messages)
                edge_parts.append(edge_messages)
            else:
                received = from_behind((face_messages, edge_messages), "blocks", -distance)
                face_parts.append(received[0])
                edge_parts.append(received[1])
        face_window = jnp.concatenate(face_parts, axis=0)
        edge_window = jnp.concatenate(edge_parts, axis=0)
        face_channels = face_window.shape[2]
        flat_faces = face_window.reshape(window_size * 6, face_channels, face_size)
        flat_edges = edge_window.reshape(window_size * 12, 1, edge_size)
        face_ghost = jnp.take(flat_faces, face_index, axis=0)
        edge_ghost = jnp.take(flat_edges, edge_index, axis=0)
        padded = jnp.zeros(
            (blocks_here, 19, edge_size + 2, edge_size + 2, edge_size + 2), jnp.float32
        )
        padded = padded.at[:, :, 1:-1, 1:-1, 1:-1].set(collided_cells)
        source_flags = jnp.ones(
            (blocks_here, edge_size + 2, edge_size + 2, edge_size + 2), jnp.int32
        )
        source_flags = source_flags.at[:, 1:-1, 1:-1, 1:-1].set(block_flags)
        for direction_code in range(18):
            offset = VELOCITY[direction_code + 1]
            region = ghost_region(offset, edge_size)
            ghost_shape = tuple((1 if component != 0 else edge_size for component in offset))
            if direction_code < 6:
                ghost_data = face_ghost[:, direction_code]
            else:
                ghost_data = edge_ghost[:, direction_code - 6]
            ghost_data = ghost_data.reshape((blocks_here, ghost_data.shape[1]) + ghost_shape)
            padded = padded.at[
                (slice(None), np.array(channel_list(direction_code ^ 1))) + region
            ].set(ghost_data)
            flag_value = (
                jnp.where(present[:, direction_code], 0, 1)
                .astype(jnp.int32)
                .reshape(blocks_here, 1, 1, 1)
            )
            source_flags = source_flags.at[(slice(None),) + region].set(
                jnp.broadcast_to(flag_value, (blocks_here,) + ghost_shape)
            )
        pdf_state = propagate(padded, source_flags, collided_cells, block_flags)
    return pdf_state.reshape(blocks_here, 19, cells_block)


def solution(mesh):
    in_specs = (P("blocks", None, None), P(), P("blocks", None), P("blocks", None))
    out_specs = P("blocks", None, None)
    return jax.shard_map(
        per_device, mesh=mesh, in_specs=in_specs, out_specs=out_specs, check_vma=False
    )
```

profile of v0, /device:TPU:0, one launch (start us, length us, event | category | flops | bytes accessed | tf_op | source)
XLA Modules:
  0.0 1978.2 jit_solution(4552881723075968303)
XLA Ops:
  0.0 36.8 %copy.456 = f32[2,19,32768]{1,0,2:T(2,128)} copy(f32[2,19,32768]{2,0,1:T(2,128)} %param.287) | data formatting | bytes 9961472 | tf_op args[0]
  36.8 52.3 %reshape.10451 = f32[32,1,38912]{2,1,0:T(1,128)} reshape(f32[32768,2,19]{2,1,0:T(2,128)} %bitcast.1219) | data formatting | bytes 9961472
  96.5 110.9 %all-to-all-done = f32[32,1,38912]{2,1,0:T(1,128)} async-done(((f32[32,1,38912]{2,1,0:T(1,128)}), f32[32,1,38912]{2,1,0:T(1,128)}, u32[]{:S(2)}, u32[]{:S(2)}) %all-to-all-start) | async-done | bytes 4980768 | tf_op jit(solution)/shard_map/all_to_all | solution.py:209
  207.9 53.5 %reduce.337 = f32[32,38912]{1,0:T(8,128)} reduce(f32[32,1,38912]{2,1,0:T(1,128)} %all-to-all-done, f32[]{:T(128)} %broadcast.6168), dimensions={1}, to_apply=%all_to_all.26.reduce_sub_computation | reduce | bytes 9961476 | tf_op jit(solution)/shard_map/all_to_all | solution.py:209
  261.4 74.2 %reshape.10452 = f32[32768,2,19]{2,1,0:T(2,128)} reshape(f32[32,38912]{1,0:T(8,128)} %reduce.337) | data formatting | bytes 9961472
  335.6 40.0 %copy.553 = f32[32,2,19,1024]{3,2,1,0:T(8,128)} copy(f32[32,2,19,1024]{2,1,3,0:T(2,128)} %bitcast.1218) | data formatting | bytes 9961472 | tf_op jit(solution)/shard_map/all_to_all | solution.py:209
  428.5 28.5 %all-to-all-done.1 = f32[32,19,1024]{2,1,0:T(8,128)} async-done(((f32[32,19,1024]{2,1,0:T(8,128)}), f32[32,19,1024]{2,1,0:T(8,128)}, u32[]{:S(2)}, u32[]{:S(2)}) %all-to-all-start.1) | async-done | bytes 2490400 | tf_op jit(solution)/shard_map/all_to_all | solution.py:211
  498.2 11.9 pad_bitcast_fusion.1
  580.5 12.9 collective-permute-start
  633.9 11.4 collective-permute-done.10
  652.4 61.1 %while.100 = (s32[]{:T(128)}, f32[1,19,34,34,34]{4,3,2,1,0:T(8,128)}, s32[5,4]{0,1:T(4,128)S(1)}, f32[5,1,1,32,32]{4,3,2,1,0:T(8,128)S(1)}, s32[]{:T(128)}, /*index=5*/s32[5]{0:T(128)S(1)}, s32[1]{0:T(128)}, s32[]{:T(128)}) while((s32[]{:T(128)}, f32[1,19,34,34,34]{4,3,2,1,0:T(8,128)}, s32[5,4]{0,1:T(4,128)S(1)}, ...), condition=%wide.while_cond.88, body=%wide.while_body.88.sunk | while | flops 1045 | bytes 20747 | solution.py:281
  713.6 61.1 %while.101 = (s32[]{:T(128)}, f32[1,19,34,34,34]{4,3,2,1,0:T(8,128)}, s32[5,4]{0,1:T(4,128)S(1)}, f32[5,1,1,32,32]{4,3,2,1,0:T(8,128)S(1)}, s32[]{:T(128)}, /*index=5*/s32[5]{0:T(128)S(1)}, s32[1]{0:T(128)}, s32[]{:T(128)}) while((s32[]{:T(128)}, f32[1,19,34,34,34]{4,3,2,1,0:T(8,128)}, s32[5,4]{0,1:T(4,128)S(1)}, ...), condition=%wide.while_cond.89, body=%wide.while_body.89.sunk | while | flops 1045 | bytes 20747 | solution.py:281
  774.8 79.6 %while.102 = (s32[]{:T(128)}, f32[1,19,34,34,34]{4,3,2,1,0:T(8,128)}, s32[5,4]{0,1:T(4,128)S(1)}, f32[5,1,32,1,32]{4,3,2,1,0:T(1,128)S(1)}, s32[]{:T(128)}, /*index=5*/s32[5]{0:T(128)S(1)}, s32[1]{0:T(128)}, s32[]{:T(128)}) while((s32[]{:T(128)}, f32[1,19,34,34,34]{4,3,2,1,0:T(8,128)}, s32[5,4]{0,1:T(4,128)S(1)}, ...), condition=%wide.while_cond.90, body=%wide.while_body.90.sunk | while | flops 1045 | bytes 20747 | solution.py:281
  782.6 8.1 dynamic-update-slice.314
  854.5 79.6 %while.103 = (s32[]{:T(128)}, f32[1,19,34,34,34]{4,3,2,1,0:T(8,128)}, s32[5,4]{0,1:T(4,128)S(1)}, f32[5,1,32,1,32]{4,3,2,1,0:T(1,128)S(1)}, s32[]{:T(128)}, /*index=5*/s32[5]{0:T(128)S(1)}, s32[1]{0:T(128)}, s32[]{:T(128)}) while((s32[]{:T(128)}, f32[1,19,34,34,34]{4,3,2,1,0:T(8,128)}, s32[5,4]{0,1:T(4,128)S(1)}, ...), condition=%wide.while_cond.91, body=%wide.while_body.91.sunk | while | flops 1045 | bytes 20747 | solution.py:281
  938.2 94.6 %while.104 = (s32[]{:T(128)}, f32[1,19,34,34,34]{4,3,2,1,0:T(8,128)}, s32[5,4]{0,1:T(4,128)S(1)}, f32[5,1,32,32,1]{4,3,2,1,0:T(8,128)}, s32[]{:T(128)}, /*index=5*/s32[5]{0:T(128)}, s32[1]{0:T(128)}, s32[]{:T(128)}) while((s32[]{:T(128)}, f32[1,19,34,34,34]{4,3,2,1,0:T(8,128)}, s32[5,4]{0,1:T(4,128)S(1)}, f32[5,1,32,32,1]{4,3,2,1,0:T(8,128)}, ...), condition=%wide.while_cond.92, body=%wide.while_body.92.sunk | while | flops 1045 | bytes 20747 | solution.py:281
  947.1 10.0 dynamic-update-slice.316
  966.1 10.0 dynamic-update-slice.316
  985.0 10.1 dynamic-update-slice.316
  1003.9 10.0 dynamic-update-slice.316
  1022.8 10.0 dynamic-update-slice.316
  1037.0 74.8 %while.105 = (s32[]{:T(128)}, f32[1,19,34,34,34]{4,3,2,1,0:T(8,128)}, s32[5,4]{0,1:T(4,128)S(1)}, f32[5,1,32,32,1]{4,3,2,1,0:T(8,128)}, s32[]{:T(128)}, /*index=5*/s32[5]{0:T(128)}, s32[1]{0:T(128)}, s32[]{:T(128)}) while((s32[]{:T(128)}, f32[1,19,34,34,34]{4,3,2,1,0:T(8,128)}, s32[5,4]{0,1:T(4,128)S(1)}, f32[5,1,32,32,1]{4,3,2,1,0:T(8,128)}, ...), condition=%wide.while_cond.93, body=%wide.while_body.93.sunk | while | flops 1045 | bytes 20747 | solution.py:281
  1134.5 17.3 add_add_fusion
  1182.7 8.3 stack.146
  1238.6 11.9 pad_bitcast_fusion
  1308.1 11.6 collective-permute-start.28
  1366.3 11.7 collective-permute-done.38
  1382.8 70.4 %while.106 = (s32[]{:T(128)}, f32[1,19,34,34,34]{4,3,2,1,0:T(8,128)}, s32[5,4]{0,1:T(4,128)}, f32[5,1,1,32,32]{4,3,2,1,0:T(8,128)S(1)}, s32[]{:T(128)}, /*index=5*/s32[5]{0:T(128)}, s32[1]{0:T(128)}, s32[]{:T(128)}) while((s32[]{:T(128)}, f32[1,19,34,34,34]{4,3,2,1,0:T(8,128)}, s32[5,4]{0,1:T(4,128)}, f32[5,1,1,32,32]{4,3,2,1,0:T(8,128)S(1)}, ...), condition=%wide.while_cond.94, body=%wide.while_body.94.sunk | while | flops 1045 | bytes 20747 | solution.py:281
  1453.3 70.5 %while.107 = (s32[]{:T(128)}, f32[1,19,34,34,34]{4,3,2,1,0:T(8,128)}, s32[5,4]{0,1:T(4,128)}, f32[5,1,1,32,32]{4,3,2,1,0:T(8,128)S(1)}, s32[]{:T(128)}, /*index=5*/s32[5]{0:T(128)}, s32[1]{0:T(128)}, s32[]{:T(128)}) while((s32[]{:T(128)}, f32[1,19,34,34,34]{4,3,2,1,0:T(8,128)}, s32[5,4]{0,1:T(4,128)}, f32[5,1,1,32,32]{4,3,2,1,0:T(8,128)S(1)}, ...), condition=%wide.while_cond.95, body=%wide.while_body.95.sunk | while | flops 1045 | bytes 20747 | solution.py:281
  1523.9 85.4 %while.108 = (s32[]{:T(128)}, f32[1,19,34,34,34]{4,3,2,1,0:T(8,128)}, s32[5,4]{0,1:T(4,128)S(1)}, f32[5,1,32,1,32]{4,3,2,1,0:T(1,128)S(1)}, s32[]{:T(128)}, /*index=5*/s32[5]{0:T(128)}, s32[1]{0:T(128)}, s32[]{:T(128)}) while((s32[]{:T(128)}, f32[1,19,34,34,34]{4,3,2,1,0:T(8,128)}, s32[5,4]{0,1:T(4,128)S(1)}, f32[5,1,32,1,32]{4,3,2,1,0:T(1,128)S(1)}, ...), condition=%wide.while_cond.96, body=%wide.while_body.96.sunk | while | flops 1045 | bytes 20747 | solution.py:281
  1532.7 8.2 dynamic-update-slice.320
  1549.8 8.2 dynamic-update-slice.320
  1566.9 8.2 dynamic-update-slice.320
  1584.0 8.2 dynamic-update-slice.320
  1601.0 8.2 dynamic-update-slice.320
  1609.4 85.3 %while.109 = (s32[]{:T(128)}, f32[1,19,34,34,34]{4,3,2,1,0:T(8,128)}, s32[5,4]{0,1:T(4,128)S(1)}, f32[5,1,32,1,32]{4,3,2,1,0:T(1,128)S(1)}, s32[]{:T(128)}, /*index=5*/s32[5]{0:T(128)}, s32[1]{0:T(128)}, s32[]{:T(128)}) while((s32[]{:T(128)}, f32[1,19,34,34,34]{4,3,2,1,0:T(8,128)}, s32[5,4]{0,1:T(4,128)S(1)}, f32[5,1,32,1,32]{4,3,2,1,0:T(1,128)S(1)}, ...), condition=%wide.while_cond.97, body=%wide.while_body.97.sunk | while | flops 1045 | bytes 20747 | solution.py:281
  1618.2 8.2 dynamic-update-slice.321
  1635.2 8.2 dynamic-update-slice.321
  1652.3 8.2 dynamic-update-slice.321
  1669.4 8.2 dynamic-update-slice.321
  1686.4 8.2 dynamic-update-slice.321
  1697.2 96.1 %while.110 = (s32[]{:T(128)}, f32[1,19,34,34,34]{4,3,2,1,0:T(8,128)}, s32[5,4]{0,1:T(4,128)S(1)}, f32[5,1,32,32,1]{4,3,2,1,0:T(8,128)S(1)}, s32[]{:T(128)}, /*index=5*/s32[5]{0:T(128)}, s32[1]{0:T(128)}, s32[]{:T(128)}) while((s32[]{:T(128)}, f32[1,19,34,34,34]{4,3,2,1,0:T(8,128)}, s32[5,4]{0,1:T(4,128)S(1)}, f32[5,1,32,32,1]{4,3,2,1,0:T(8,128)S(1)}, ...), condition=%wide.while_cond.98, body=%wide.while_body.98.sunk | while | flops 1045 | bytes 20747 | solution.py:281
  1706.3 10.1 dynamic-update-slice.322
  1725.5 10.1 dynamic-update-slice.322
  1744.7 10.1 dynamic-update-slice.322
  1764.0 10.1 dynamic-update-slice.322
  1783.2 10.1 dynamic-update-slice.322
  1796.7 76.9 %while.111 = (s32[]{:T(128)}, f32[1,19,34,34,34]{4,3,2,1,0:T(8,128)}, s32[5,4]{0,1:T(4,128)S(1)}, f32[5,1,32,32,1]{4,3,2,1,0:T(8,128)S(1)}, s32[]{:T(128)}, /*index=5*/s32[5]{0:T(128)}, s32[1]{0:T(128)}, s32[]{:T(128)}) while((s32[]{:T(128)}, f32[1,19,34,34,34]{4,3,2,1,0:T(8,128)}, s32[5,4]{0,1:T(4,128)S(1)}, f32[5,1,32,32,1]{4,3,2,1,0:T(8,128)S(1)}, ...), condition=%wide.while_cond.99, body=%wide.while_body.99.sunk | while | flops 1045 | bytes 20747 | solution.py:281
  (923 shorter events, 1278.5 us)
Async XLA Ops:
  89.0 118.4 %all-to-all-start = ((f32[32,1,38912]{2,1,0:T(1,128)}), f32[32,1,38912]{2,1,0:T(1,128)}, u32[]{:S(2)}, u32[]{:S(2)}) async-start(f32[32,1,38912]{2,1,0:T(1,128)} %reshape.10451), calls=%async_computation | async-start | bytes 9961472 | tf_op jit(solution)/shard_map/all_to_all | solution.py:209
  381.2 75.8 %all-to-all-start.1 = ((f32[32,19,1024]{2,1,0:T(8,128)}), f32[32,19,1024]{2,1,0:T(8,128)}, u32[]{:S(2)}, u32[]{:S(2)}) async-start(f32[32,19,1024]{2,1,0:T(8,128)} %broadcast_select_fusion.4), calls=%async_computation.1 | async-start | bytes 6291456 | tf_op jit(solution)/shard_map/all_to_all | solution.py:211
  513.8 32.7 %collective-permute-start.14 = (f32[1,384]{1,0:T(1,128)S(1)}, f32[1,384]{1,0:T(1,128)S(1)}, u32[]{:S(2)}, u32[]{:S(2)}) collective-permute-start(f32[1,384]{1,0:T(1,128)S(1)} %bitcast.1250), channel_id=1, source_target_pairs={{0,7},{1,8},{2,9},{3,10},{4,11},{5,12},{6,13},{7,14},{8,15},{9,16}... | collective-permute-start | bytes 4616 | tf_op jit(solution)/shard_map/ppermute | solution.py:60
  517.2 32.8 %collective-permute-start.15 = (f32[1,384]{1,0:T(1,128)S(1)}, f32[1,384]{1,0:T(1,128)S(1)}, u32[]{:S(2)}, u32[]{:S(2)}) collective-permute-start(f32[1,384]{1,0:T(1,128)S(1)} %bitcast.1251), channel_id=1, source_target_pairs={{0,6},{1,7},{2,8},{3,9},{4,10},{5,11},{6,12},{7,13},{8,14},{9,15},... | collective-permute-start | bytes 4616 | tf_op jit(solution)/shard_map/ppermute | solution.py:60
  519.2 32.0 %collective-permute-start.16 = (f32[1,384]{1,0:T(1,128)S(1)}, f32[1,384]{1,0:T(1,128)S(1)}, u32[]{:S(2)}, u32[]{:S(2)}) collective-permute-start(f32[1,384]{1,0:T(1,128)S(1)} %bitcast.1252), channel_id=1, source_target_pairs={{0,5},{1,6},{2,7},{3,8},{4,9},{5,10},{6,11},{7,12},{8,13},{9,14},{... | collective-permute-start | bytes 4616 | tf_op jit(solution)/shard_map/ppermute | solution.py:60
  521.6 31.0 %collective-permute-start.17 = (f32[1,384]{1,0:T(1,128)S(1)}, f32[1,384]{1,0:T(1,128)S(1)}, u32[]{:S(2)}, u32[]{:S(2)}) collective-permute-start(f32[1,384]{1,0:T(1,128)S(1)} %bitcast.1253), channel_id=1, source_target_pairs={{0,4},{1,5},{2,6},{3,7},{4,8},{5,9},{6,10},{7,11},{8,12},{9,13},{1... | collective-permute-start | bytes 4616 | tf_op jit(solution)/shard_map/ppermute | solution.py:60
  524.7 34.0 %collective-permute-start.18 = (f32[1,384]{1,0:T(1,128)S(1)}, f32[1,384]{1,0:T(1,128)S(1)}, u32[]{:S(2)}, u32[]{:S(2)}) collective-permute-start(f32[1,384]{1,0:T(1,128)S(1)} %bitcast.1254), channel_id=1, source_target_pairs={{0,3},{1,4},{2,5},{3,6},{4,7},{5,8},{6,9},{7,10},{8,11},{9,12},{10... | collective-permute-start | bytes 4616 | tf_op jit(solution)/shard_map/ppermute | solution.py:60
  546.6 13.4 collective-permute-start.19
  549.9 11.4 collective-permute-start.20
  551.2 11.4 collective-permute-start.21
  552.6 11.4 collective-permute-start.22
  558.7 21.8 %collective-permute-start.23 = (f32[1,384]{1,0:T(1,128)S(1)}, f32[1,384]{1,0:T(1,128)}, u32[]{:S(2)}, u32[]{:S(2)}) collective-permute-start(f32[1,384]{1,0:T(1,128)S(1)} %bitcast.1259), channel_id=1, source_target_pairs={{3,0},{4,1},{5,2},{6,3},{7,4},{8,5},{9,6},{10,7},{11,8},{12,9},{13... | collective-permute-start | bytes 4616 | tf_op jit(solution)/shard_map/ppermute | solution.py:60
  560.0 33.4 %collective-permute-start.24 = (f32[1,384]{1,0:T(1,128)S(1)}, f32[1,384]{1,0:T(1,128)}, u32[]{:S(2)}, u32[]{:S(2)}) collective-permute-start(f32[1,384]{1,0:T(1,128)S(1)} %bitcast.1260), channel_id=1, source_target_pairs={{4,0},{5,1},{6,2},{7,3},{8,4},{9,5},{10,6},{11,7},{12,8},{13,9},{1... | collective-permute-start | bytes 4616 | tf_op jit(solution)/shard_map/ppermute | solution.py:60
  561.3 38.2 %collective-permute-start.25 = (f32[1,384]{1,0:T(1,128)S(1)}, f32[1,384]{1,0:T(1,128)}, u32[]{:S(2)}, u32[]{:S(2)}) collective-permute-start(f32[1,384]{1,0:T(1,128)S(1)} %bitcast.1261), channel_id=1, source_target_pairs={{5,0},{6,1},{7,2},{8,3},{9,4},{10,5},{11,6},{12,7},{13,8},{14,9},{... | collective-permute-start | bytes 4616 | tf_op jit(solution)/shard_map/ppermute | solution.py:60
  562.6 41.1 %collective-permute-start.26 = (f32[1,384]{1,0:T(1,128)S(1)}, f32[1,384]{1,0:T(1,128)}, u32[]{:S(2)}, u32[]{:S(2)}) collective-permute-start(f32[1,384]{1,0:T(1,128)S(1)} %bitcast.1262), channel_id=1, source_target_pairs={{6,0},{7,1},{8,2},{9,3},{10,4},{11,5},{12,6},{13,7},{14,8},{15,9},... | collective-permute-start | bytes 4616 | tf_op jit(solution)/shard_map/ppermute | solution.py:60
  563.9 42.3 %collective-permute-start.27 = (f32[1,384]{1,0:T(1,128)S(1)}, f32[1,384]{1,0:T(1,128)}, u32[]{:S(2)}, u32[]{:S(2)}) collective-permute-start(f32[1,384]{1,0:T(1,128)S(1)} %bitcast.1263), channel_id=1, source_target_pairs={{7,0},{8,1},{9,2},{10,3},{11,4},{12,5},{13,6},{14,7},{15,8},{16,9}... | collective-permute-start | bytes 4616 | tf_op jit(solution)/shard_map/ppermute | solution.py:60
  580.5 34.0 %collective-permute-start = (f32[1,6,5,1024]{3,1,2,0:T(8,128)S(1)}, f32[1,6,5,1024]{3,1,2,0:T(8,128)S(1)}, u32[]{:S(2)}, u32[]{:S(2)}) collective-permute-start(f32[1,6,5,1024]{3,1,2,0:T(8,128)S(1)} %stack.126), channel_id=1, source_target_pairs={{0,7},{1,8},{2,9},{3,10},{4,11},{5,12},{6,13},{7,14},{8,15},{9,16}... | collective-permute-start | bytes 368648 | tf_op jit(solution)/shard_map/ppermute | solution.py:60
  593.4 25.6 %collective-permute-start.1 = (f32[1,6,5,1024]{3,1,2,0:T(8,128)S(1)}, f32[1,6,5,1024]{3,1,2,0:T(8,128)S(1)}, u32[]{:S(2)}, u32[]{:S(2)}) collective-permute-start(f32[1,6,5,1024]{3,1,2,0:T(8,128)S(1)} %stack.126), channel_id=1, source_target_pairs={{0,6},{1,7},{2,8},{3,9},{4,10},{5,11},{6,12},{7,13},{8,14},{9,15},... | collective-permute-start | bytes 368648 | tf_op jit(solution)/shard_map/ppermute | solution.py:60
  599.5 20.9 %collective-permute-start.2 = (f32[1,6,5,1024]{3,1,2,0:T(8,128)S(1)}, f32[1,6,5,1024]{3,1,2,0:T(8,128)S(1)}, u32[]{:S(2)}, u32[]{:S(2)}) collective-permute-start(f32[1,6,5,1024]{3,1,2,0:T(8,128)S(1)} %stack.126), channel_id=1, source_target_pairs={{0,5},{1,6},{2,7},{3,8},{4,9},{5,10},{6,11},{7,12},{8,13},{9,14},{... | collective-permute-start | bytes 368648 | tf_op jit(solution)/shard_map/ppermute | solution.py:60
  603.7 18.0 collective-permute-start.3
  606.2 16.8 collective-permute-start.4
  624.4 20.9 %collective-permute-start.10 = (f32[1,6,5,1024]{3,1,2,0:T(8,128)S(1)}, f32[1,6,5,1024]{3,1,2,0:T(8,128)S(1)}, u32[]{:S(2)}, u32[]{:S(2)}) collective-permute-start(f32[1,6,5,1024]{3,1,2,0:T(8,128)S(1)} %stack.126), channel_id=1, source_target_pairs={{4,0},{5,1},{6,2},{7,3},{8,4},{9,5},{10,6},{11,7},{12,8},{13,9},{1... | collective-permute-start | bytes 368648 | tf_op jit(solution)/shard_map/ppermute | solution.py:60
  625.7 21.0 %collective-permute-start.11 = (f32[1,6,5,1024]{3,1,2,0:T(8,128)S(1)}, f32[1,6,5,1024]{3,1,2,0:T(8,128)S(1)}, u32[]{:S(2)}, u32[]{:S(2)}) collective-permute-start(f32[1,6,5,1024]{3,1,2,0:T(8,128)S(1)} %stack.126), channel_id=1, source_target_pairs={{5,0},{6,1},{7,2},{8,3},{9,4},{10,5},{11,6},{12,7},{13,8},{14,9},{... | collective-permute-start | bytes 368648 | tf_op jit(solution)/shard_map/ppermute | solution.py:60
  627.0 19.7 collective-permute-start.12
  631.6 15.2 collective-permute-start.13
  1254.2 20.8 %collective-permute-start.42 = (f32[1,384]{1,0:T(1,128)S(1)}, f32[1,384]{1,0:T(1,128)S(1)}, u32[]{:S(2)}, u32[]{:S(2)}) collective-permute-start(f32[1,384]{1,0:T(1,128)S(1)} %bitcast.1265), channel_id=1, source_target_pairs={{0,7},{1,8},{2,9},{3,10},{4,11},{5,12},{6,13},{7,14},{8,15},{9,16}... | collective-permute-start | bytes 4616 | tf_op jit(solution)/shard_map/ppermute | solution.py:60
  1257.2 21.5 %collective-permute-start.43 = (f32[1,384]{1,0:T(1,128)S(1)}, f32[1,384]{1,0:T(1,128)S(1)}, u32[]{:S(2)}, u32[]{:S(2)}) collective-permute-start(f32[1,384]{1,0:T(1,128)S(1)} %bitcast.1266), channel_id=1, source_target_pairs={{0,6},{1,7},{2,8},{3,9},{4,10},{5,11},{6,12},{7,13},{8,14},{9,15},... | collective-permute-start | bytes 4616 | tf_op jit(solution)/shard_map/ppermute | solution.py:60
  1263.8 16.1 collective-permute-start.44
  1267.5 13.8 collective-permute-start.45
  1270.0 18.7 collective-permute-start.46
  1275.0 15.0 collective-permute-start.47
  1278.7 12.6 collective-permute-start.48
  1280.0 12.6 collective-permute-start.49
  1281.3 12.6 collective-permute-start.50
  1288.7 19.4 collective-permute-start.51
  1290.0 29.8 %collective-permute-start.52 = (f32[1,384]{1,0:T(1,128)S(1)}, f32[1,384]{1,0:T(1,128)}, u32[]{:S(2)}, u32[]{:S(2)}) collective-permute-start(f32[1,384]{1,0:T(1,128)S(1)} %bitcast.1275), channel_id=1, source_target_pairs={{4,0},{5,1},{6,2},{7,3},{8,4},{9,5},{10,6},{11,7},{12,8},{13,9},{1... | collective-permute-start | bytes 4616 | tf_op jit(solution)/shard_map/ppermute | solution.py:60
  1291.3 34.5 %collective-permute-start.53 = (f32[1,384]{1,0:T(1,128)S(1)}, f32[1,384]{1,0:T(1,128)}, u32[]{:S(2)}, u32[]{:S(2)}) collective-permute-start(f32[1,384]{1,0:T(1,128)S(1)} %bitcast.1276), channel_id=1, source_target_pairs={{5,0},{6,1},{7,2},{8,3},{9,4},{10,5},{11,6},{12,7},{13,8},{14,9},{... | collective-permute-start | bytes 4616 | tf_op jit(solution)/shard_map/ppermute | solution.py:60
  1292.6 37.4 %collective-permute-start.54 = (f32[1,384]{1,0:T(1,128)S(1)}, f32[1,384]{1,0:T(1,128)}, u32[]{:S(2)}, u32[]{:S(2)}) collective-permute-start(f32[1,384]{1,0:T(1,128)S(1)} %bitcast.1277), channel_id=1, source_target_pairs={{6,0},{7,1},{8,2},{9,3},{10,4},{11,5},{12,6},{13,7},{14,8},{15,9},... | collective-permute-start | bytes 4616 | tf_op jit(solution)/shard_map/ppermute | solution.py:60
  1293.9 38.6 %collective-permute-start.55 = (f32[1,384]{1,0:T(1,128)S(1)}, f32[1,384]{1,0:T(1,128)}, u32[]{:S(2)}, u32[]{:S(2)}) collective-permute-start(f32[1,384]{1,0:T(1,128)S(1)} %bitcast.1278), channel_id=1, source_target_pairs={{7,0},{8,1},{9,2},{10,3},{11,4},{12,5},{13,6},{14,7},{15,8},{16,9}... | collective-permute-start | bytes 4616 | tf_op jit(solution)/shard_map/ppermute | solution.py:60
  1308.1 38.8 %collective-permute-start.28 = (f32[1,6,5,1024]{3,1,2,0:T(8,128)S(1)}, f32[1,6,5,1024]{3,1,2,0:T(8,128)S(1)}, u32[]{:S(2)}, u32[]{:S(2)}) collective-permute-start(f32[1,6,5,1024]{3,1,2,0:T(8,128)S(1)} %stack.147), channel_id=1, source_target_pairs={{0,7},{1,8},{2,9},{3,10},{4,11},{5,12},{6,13},{7,14},{8,15},{9,16}... | collective-permute-start | bytes 368648 | tf_op jit(solution)/shard_map/ppermute | solution.py:60
  1319.8 31.7 %collective-permute-start.29 = (f32[1,6,5,1024]{3,1,2,0:T(8,128)S(1)}, f32[1,6,5,1024]{3,1,2,0:T(8,128)S(1)}, u32[]{:S(2)}, u32[]{:S(2)}) collective-permute-start(f32[1,6,5,1024]{3,1,2,0:T(8,128)S(1)} %stack.147), channel_id=1, source_target_pairs={{0,6},{1,7},{2,8},{3,9},{4,10},{5,11},{6,12},{7,13},{8,14},{9,15},... | collective-permute-start | bytes 368648 | tf_op jit(solution)/shard_map/ppermute | solution.py:60
  1325.8 27.2 %collective-permute-start.30 = (f32[1,6,5,1024]{3,1,2,0:T(8,128)S(1)}, f32[1,6,5,1024]{3,1,2,0:T(8,128)S(1)}, u32[]{:S(2)}, u32[]{:S(2)}) collective-permute-start(f32[1,6,5,1024]{3,1,2,0:T(8,128)S(1)} %stack.147), channel_id=1, source_target_pairs={{0,5},{1,6},{2,7},{3,8},{4,9},{5,10},{6,11},{7,12},{8,13},{9,14},{... | collective-permute-start | bytes 368648 | tf_op jit(solution)/shard_map/ppermute | solution.py:60
  1330.0 24.3 %collective-permute-start.31 = (f32[1,6,5,1024]{3,1,2,0:T(8,128)S(1)}, f32[1,6,5,1024]{3,1,2,0:T(8,128)S(1)}, u32[]{:S(2)}, u32[]{:S(2)}) collective-permute-start(f32[1,6,5,1024]{3,1,2,0:T(8,128)S(1)} %stack.147), channel_id=1, source_target_pairs={{0,4},{1,5},{2,6},{3,7},{4,8},{5,9},{6,10},{7,11},{8,12},{9,13},{1... | collective-permute-start | bytes 368648 | tf_op jit(solution)/shard_map/ppermute | solution.py:60
  1332.6 23.1 %collective-permute-start.32 = (f32[1,6,5,1024]{3,1,2,0:T(8,128)S(1)}, f32[1,6,5,1024]{3,1,2,0:T(8,128)S(1)}, u32[]{:S(2)}, u32[]{:S(2)}) collective-permute-start(f32[1,6,5,1024]{3,1,2,0:T(8,128)S(1)} %stack.147), channel_id=1, source_target_pairs={{0,3},{1,4},{2,5},{3,6},{4,7},{5,8},{6,9},{7,10},{8,11},{9,12},{10... | collective-permute-start | bytes 368648 | tf_op jit(solution)/shard_map/ppermute | solution.py:60
  1357.0 20.9 %collective-permute-start.38 = (f32[1,6,5,1024]{3,1,2,0:T(8,128)S(1)}, f32[1,6,5,1024]{3,1,2,0:T(8,128)S(1)}, u32[]{:S(2)}, u32[]{:S(2)}) collective-permute-start(f32[1,6,5,1024]{3,1,2,0:T(8,128)S(1)} %stack.147), channel_id=1, source_target_pairs={{4,0},{5,1},{6,2},{7,3},{8,4},{9,5},{10,6},{11,7},{12,8},{13,9},{1... | collective-permute-start | bytes 368648 | tf_op jit(solution)/shard_map/ppermute | solution.py:60
  1358.3 21.0 %collective-permute-start.39 = (f32[1,6,5,1024]{3,1,2,0:T(8,128)S(1)}, f32[1,6,5,1024]{3,1,2,0:T(8,128)S(1)}, u32[]{:S(2)}, u32[]{:S(2)}) collective-permute-start(f32[1,6,5,1024]{3,1,2,0:T(8,128)S(1)} %stack.147), channel_id=1, source_target_pairs={{5,0},{6,1},{7,2},{8,3},{9,4},{10,5},{11,6},{12,7},{13,8},{14,9},{... | collective-permute-start | bytes 368648 | tf_op jit(solution)/shard_map/ppermute | solution.py:60
  1359.7 19.7 collective-permute-start.40
  1363.8 15.6 collective-permute-start.41
  (101 other events, 4089.5 us)
where the time goes:
time: 2010 us; the launch traced here: 1980 us
  local copies, waits for them, and re-layouts  1160 us (58%)
  other arithmetic  434 us (22%)
  waiting for transfers between devices  174 us (9%)
  starting transfers between devices  166 us (8%)
  matrix products  25.6 us (1%)
    scatter x240, local copies, waits for them, and re-layouts  621 us
    scatter x120, other arithmetic  313 us
    unnamed x237, local copies, waits for them, and re-layouts  202 us
    ppermute x56, starting transfers between devices, from_behind(): return lax.ppermute(shard, axis, pairs)  154 us
    all_to_all x1, waiting for transfers between devices, per_device(): lax.all_to_all(old_pdfs, 'blocks', split_axis=2, concat_axis=0, tiled=True)  111 us
    another operation x40, local copies, waits for them, and re-layouts, propagate(): return jnp.stack(results, axis=1)  64.9 us
    gather x12, local copies, waits for them, and re-layouts, per_device(): collided_cells[:, np.array(channel_list(direction_code))][layer_cells]  59.7 us
    all_to_all x1, other arithmetic, per_device(): lax.all_to_all(old_pdfs, 'blocks', split_axis=2, concat_axis=0, tiled=True)  53.5 us
  transfers between devices with their start and end apart: 58, of which 10 were waited for; matrix products, arithmetic and copies ran while one was open for 5% of the time, Pallas kernels for 0%

commit v1 on v0

v1 whole, which is shorter than its diff:
```python
import functools

import jax
import jax.numpy as jnp
import numpy as np
from jax import lax
from jax.experimental import pallas as pl
from jax.experimental.pallas import tpu as pltpu
from jax.sharding import PartitionSpec as P

EDGE = 32
STEPS = 2
MESH = pl.DeviceIdType.MESH

VELOCITY = (
    (0, 0, 0),
    (1, 0, 0),
    (-1, 0, 0),
    (0, 1, 0),
    (0, -1, 0),
    (0, 0, 1),
    (0, 0, -1),
    (1, 1, 0),
    (-1, -1, 0),
    (1, -1, 0),
    (-1, 1, 0),
    (1, 0, 1),
    (-1, 0, -1),
    (1, 0, -1),
    (-1, 0, 1),
    (0, 1, 1),
    (0, -1, -1),
    (0, 1, -1),
    (0, -1, 1),
)
WEIGHT_LIST = (1.0 / 3.0,) + (1.0 / 18.0,) * 6 + (1.0 / 36.0,) * 12
RELAXATION = (
    0.0,
    0.0,
    0.0,
    0.0,
    1.19,
    1.4,
    1.2,
    1.2,
    1.2,
    1.6,
    1.6,
    1.6,
    1.6,
    1.6,
    1.4,
    1.4,
    1.98,
    1.98,
    1.98,
)
INLET_SPEED = (0.0, 0.0, 0.05)

X_PLUS, X_MINUS = (1, 7, 9, 11, 13), (2, 8, 10, 12, 14)
Y_PLUS, Y_MINUS = (3, 7, 10, 15, 17), (4, 8, 9, 16, 18)
Z_PLUS, Z_MINUS = (5, 11, 14, 15, 18), (6, 12, 13, 16, 17)
ORBITS = ((0,), (1, 2), (3, 4), (5, 6), (7, 8, 9, 10), (11, 12, 13, 14), (15, 16, 17, 18))


def collision_table():
    lattice = np.array(VELOCITY) * 1.0
    along_x, along_y, along_z = (lattice[:, 0], lattice[:, 1], lattice[:, 2])
    squared = along_x * along_x + along_y * along_y + along_z * along_z
    monomials = [
        np.ones(19),
        along_x,
        along_y,
        along_z,
        squared,
        squared * squared,
        squared * along_x,
        squared * along_y,
        squared * along_z,
        3.0 * along_x * along_x - squared,
        along_y * along_y - along_z * along_z,
        along_x * along_y,
        along_y * along_z,
        along_x * along_z,
        squared * (3.0 * along_x * along_x - squared),
        squared * (along_y * along_y - along_z * along_z),
        (along_y * along_y - along_z * along_z) * along_x,
        (along_z * along_z - along_x * along_x) * along_y,
        (along_x * along_x - along_y * along_y) * along_z,
    ]
    orthonormal = []
    for vector in monomials:
        for earlier in orthonormal:
            vector = vector - np.dot(vector, earlier) * earlier
        orthonormal.append(vector / np.sqrt(np.dot(vector, vector)))
    stacked = np.stack(orthonormal)
    return stacked.T * np.array(RELAXATION) @ stacked


def opposite(index_value):
    if index_value == 0:
        return 0
    return index_value + 1 if index_value % 2 == 1 else index_value - 1


def code_of(offset):
    return VELOCITY.index(tuple(offset)) - 1


def collision_blocks():
    matrix = collision_table().astype(np.float32).astype(np.float64)
    even = [[float(np.mean([matrix[a[0], b] for b in group])) for group in ORBITS] for a in ORBITS]
    odd = []
    for axis in range(3):
        groups = [g for g in ORBITS if any(VELOCITY[b][axis] for b in g)]
        rows = []
        for a in groups:
            first = next(c for c in a if VELOCITY[c][axis] > 0)
            rows.append(
                [float(np.mean([VELOCITY[b][axis] * matrix[first, b] for b in g])) for g in groups]
            )
        odd.append(rows)
    mixed = []
    for group in ORBITS[4:]:
        signs = [1.0, 1.0, -1.0, -1.0]
        mixed.append(float(np.mean([s * matrix[group[0], b] for s, b in zip(signs, group)])))
    return even, odd, mixed


def dot(coefficients, terms):
    total = None
    for coefficient, term in zip(coefficients, terms):
        part = term * np.float32(coefficient)
        total = part if total is None else total + part
    return total


def collide(f):
    even, odd, mixed = collision_blocks()
    pair_sum = [f[i] + f[i + 1] for i in (1, 3, 5)]
    pair_dif = [f[i] - f[i + 1] for i in (1, 3, 5)]
    quad_sum, quad_mix, quad_one, quad_two = [], [], [], []
    for i in (7, 11, 15):
        sum_a, sum_b = f[i] + f[i + 1], f[i + 2] + f[i + 3]
        dif_a, dif_b = f[i] - f[i + 1], f[i + 2] - f[i + 3]
        quad_sum.append(sum_a + sum_b)
        quad_mix.append(sum_a - sum_b)
        quad_one.append(dif_a + dif_b)
        quad_two.append(dif_a - dif_b)
    odd_terms = [
        [pair_dif[0], quad_one[0], quad_one[1]],
        [pair_dif[1], quad_two[0], quad_one[2]],
        [pair_dif[2], quad_two[1], quad_two[2]],
    ]
    rho = f[0] + (pair_sum[0] + pair_sum[1] + pair_sum[2]) + (quad_sum[0] + quad_sum[1] + quad_sum[2])
    j = [t[0] + t[1] + t[2] for t in odd_terms]
    sq = [c * c for c in j]
    base = rho - 1.5 * (sq[0] + sq[1] + sq[2])
    sq45 = [4.5 * s for s in sq]
    w0, w1, w2 = 1.0 / 3.0, 1.0 / 18.0, 1.0 / 36.0
    even_terms = [f[0] - w0 * base]
    for a in range(3):
        even_terms.append(pair_sum[a] - (2.0 * w1) * (base + sq45[a]))
    for q, (a, b) in enumerate(((0, 1), (0, 2), (1, 2))):
        even_terms.append(quad_sum[q] - (4.0 * w2) * (base + sq45[a] + sq45[b]))
    mix = [
        (quad_mix[q] - j[a] * j[b]) * np.float32(mixed[q])
        for q, (a, b) in enumerate(((0, 1), (0, 2), (1, 2)))
    ]
    odd_out = []
    for a in range(3):
        third = j[a] * np.float32(1.0 / 3.0)
        terms = [t - third for t in odd_terms[a]]
        odd_out.append([dot(row, terms) for row in odd[a]])
    even_out = [dot(row, even_terms) for row in even]
    out = [f[0] - even_out[0]]
    for a in range(3):
        out.append(f[1 + 2 * a] - (even_out[1 + a] + odd_out[a][0]))
        out.append(f[2 + 2 * a] - (even_out[1 + a] - odd_out[a][0]))
    for q, (one, two) in enumerate(
        (
            (odd_out[0][1], odd_out[1][1]),
            (odd_out[0][2], odd_out[2][1]),
            (odd_out[1][2], odd_out[2][2]),
        )
    ):
        i = 7 + 4 * q
        plus, minus = even_out[4 + q] + mix[q], even_out[4 + q] - mix[q]
        both, apart = one + two, one - two
        out.append(f[i] - (plus + both))
        out.append(f[i + 1] - (plus - both))
        out.append(f[i + 2] - (minus + apart))
        out.append(f[i + 3] - (minus - apart))
    return out


def positions():
    lane = lax.broadcasted_iota(jnp.int32, (8, 128), 1)
    sub = lax.broadcasted_iota(jnp.int32, (8, 128), 0)
    return lane, sub


def shift_y(v, step, ghost, lane, sub):
    if step > 0:
        moved = pltpu.roll(v, 32, 1)
        out = jnp.where(lane < 32, pltpu.roll(moved, 1, 0), moved)
        return jnp.where((lane < 32) & (sub == 0), ghost, out)
    moved = pltpu.roll(v, 96, 1)
    out = jnp.where(lane >= 96, pltpu.roll(moved, 7, 0), moved)
    return jnp.where((lane >= 96) & (sub == 7), ghost, out)


def shift_z(v, step, ghost, z):
    moved = pltpu.roll(v, 1 if step > 0 else 127, 1)
    return jnp.where(z == (0 if step > 0 else 31), ghost, moved)


def unpack_ghosts(nbr, rxy, gy):
    lane, _ = positions()
    jy = jnp.maximum(nbr[0, 2], nbr[0, 3]) & 3
    jd = jnp.maximum(jnp.maximum(nbr[0, 6], nbr[0, 7]), jnp.maximum(nbr[0, 8], nbr[0, 9])) & 3
    for k in range(5):
        packed = rxy[jy, 5 + k]
        for g in range(4):
            low = pltpu.roll(packed, (128 - 32 * g) % 128, 1)
            high = pltpu.roll(packed, (96 - 32 * g) % 128, 1)
            gy[k, 1 + 8 * g : 9 + 8 * g, :] = jnp.where(lane < 64, low, high)
    for channel in (7, 8, 9, 10):
        cx, cy, _ = VELOCITY[channel]
        kx = (X_PLUS if cx > 0 else X_MINUS).index(channel)
        ky = (Y_PLUS if cy > 0 else Y_MINUS).index(channel)
        plane = rxy[jd, kx]
        row = pltpu.roll(plane, 32 if cy > 0 else 96, 1)
        row = row[7:8, :] if cy > 0 else row[0:1, :]
        spot = 0 if cx > 0 else 33
        gy[ky, spot : spot + 1, :] = row


def pull(x, nbr, c, rxy, rb, ra, flags, gy):
    lane, sub = positions()
    z = lane & 31
    jx = jnp.maximum(nbr[0, 0], nbr[0, 1]) & 3

    def wall(offset):
        return jnp.where(nbr[0, code_of(offset)] >= 0, 0, 1).astype(jnp.int32)

    def spot(offset):
        return nbr[0, code_of(offset)] & 3

    own = flags[x]
    values = [c[x, i] for i in range(19)]
    j = []
    for axis in range(3):
        plus = sum(values[i] for i in range(19) if VELOCITY[i][axis] > 0)
        minus = sum(values[i] for i in range(19) if VELOCITY[i][axis] < 0)
        j.append(plus - minus)
    calm = 1.0 - 1.5 * (j[0] * j[0] + j[1] * j[1] + j[2] * j[2])
    inlet_square = sum(p * p for p in INLET_SPEED)
    out = [jnp.where(own == 0, values[0], 0.0)]
    for i in range(1, 19):
        cx, cy, cz = VELOCITY[i]
        if cx:
            outside = x == (0 if cx > 0 else EDGE - 1)
            from_x = jnp.clip(x - cx, 0, EDGE - 1)
            kx = (X_PLUS if cx > 0 else X_MINUS).index(i)
            v = jnp.where(outside, rxy[jx, kx], c[from_x, i])
            kind = jnp.where(outside, wall((-cx, 0, 0)), flags[from_x])
        else:
            v, kind = values[i], own
        if cz:
            beyond = rb if cz > 0 else ra
            kz = (Z_PLUS if cz > 0 else Z_MINUS).index(i)
            block, blocked = spot((0, 0, -cz)), wall((0, 0, -cz))
            at = x
            if cx:
                block = jnp.where(outside, spot((-cx, 0, -cz)), block)
                blocked = jnp.where(outside, wall((-cx, 0, -cz)), blocked)
                at = (x - cx) & 31
            message = beyond[block, kz]
            amount = (128 - at) & 127 if cz > 0 else 31 - at
            v = shift_z(v, cz, pltpu.roll(message, amount, 1), z)
            kind = shift_z(kind, cz, blocked, z)
        if cy:
            ky = (Y_PLUS if cy > 0 else Y_MINUS).index(i)
            row = jnp.broadcast_to(gy[ky, pl.ds(x - cx + 1, 1), :], (8, 128))
            blocked = wall((0, -cy, 0))
            if cx:
                blocked = jnp.where(outside, wall((-cx, -cy, 0)), blocked)
            if cz:
                corner = beyond[spot((0, -cy, -cz)), kz]
                target = (0 if cy > 0 else 96) + (0 if cz > 0 else 31)
                source = (96 if cy > 0 else 0) + x
                corner = pltpu.roll(corner, (target - source + 256) & 127, 1)
                corner = corner[7:8, :] if cy > 0 else corner[0:1, :]
                row = shift_z(row, cz, jnp.broadcast_to(corner, (8, 128)), z)
                blocked = jnp.where(z == (0 if cz > 0 else 31), wall((0, -cy, -cz)), blocked)
            v = shift_y(v, cy, row, lane, sub)
            kind = shift_y(kind, cy, blocked, lane, sub)
        weight = WEIGHT_LIST[i]
        along = sum(a * b for a, b in zip(VELOCITY[i], INLET_SPEED))
        inlet = weight * (1.0 + 3.0 * along + 4.5 * along * along - 1.5 * inlet_square)
        speed = sum(a * b for a, b in zip(VELOCITY[i], j) if a)
        outlet = weight * (calm + speed * (3.0 + 4.5 * speed))
        new = jnp.where(
            kind == 0,
            v,
            jnp.where(kind == 1, values[opposite(i)], jnp.where(kind == 2, np.float32(inlet), outlet)),
        )
        out.append(jnp.where(own == 0, new, 0.0))
    return out


def note_faces(x, nbr, collided, zu, zd, rows):
    lane, _ = positions()
    here = (lane & 31) == x
    for k in range(5):
        up = pltpu.roll(collided[Z_PLUS[k]], (x + 97) & 127, 1)
        zu[k] = jnp.where(here, up, zu[k])
        zd[k] = jnp.where(here, pltpu.roll(collided[Z_MINUS[k]], x, 1), zd[k])
        high = collided[Y_PLUS[k]][7:8, :]
        low = collided[Y_MINUS[k]][0:1, :]
        rows[k, pl.ds(x, 1), :] = jnp.where(nbr[0, 2] >= 0, high, low)


def finish_faces(nbr, c, rows, xy):
    lane, _ = positions()
    ahead_x, ahead_y = nbr[0, 0] >= 0, nbr[0, 2] >= 0
    for k in range(5):
        xy[k] = jnp.where(ahead_x, c[EDGE - 1, X_PLUS[k]], c[0, X_MINUS[k]])
        packed = jnp.zeros((8, 128), jnp.float32)
        for g in range(4):
            part = rows[k, 8 * g : 8 * g + 8, :]
            high = pltpu.roll(part, (32 * (g + 1)) % 128, 1)
            low = pltpu.roll(part, 32 * g, 1)
            packed = jnp.where((lane >> 5) == g, jnp.where(ahead_y, high, low), packed)
        xy[5 + k] = packed


def first_kernel(nbr, f, c, xy, zu, zd, rows):
    zu[...] = jnp.zeros_like(zu)
    zd[...] = jnp.zeros_like(zd)

    def plane(x, carry):
        collided = collide([f[x, i] for i in range(19)])
        for i in range(19):
            c[x, i] = collided[i]
        note_faces(x, nbr, collided, zu, zd, rows)
        return carry

    lax.fori_loop(0, EDGE, plane, 0)
    finish_faces(nbr, c, rows, xy)


def middle_kernel(nbr, flags, c_in, rxy, rb, ra, c, xy, zu, zd, rows, gy):
    zu[...] = jnp.zeros_like(zu)
    zd[...] = jnp.zeros_like(zd)
    unpack_ghosts(nbr, rxy, gy)

    def plane(x, carry):
        collided = collide(pull(x, nbr, c_in, rxy, rb, ra, flags, gy))
        for i in range(19):
            c[x, i] = collided[i]
        note_faces(x, nbr, collided, zu, zd, rows)
        return carry

    lax.fori_loop(0, EDGE, plane, 0)
    finish_faces(nbr, c, rows, xy)


def last_kernel(nbr, flags, c_in, rxy, rb, ra, out, gy, lines):
    unpack_ghosts(nbr, rxy, gy)

    def plane(x, carry):
        f = pull(x, nbr, c_in, rxy, rb, ra, flags, gy)
        for i in range(19):
            lines[8 * i : 8 * i + 8, :] = f[i]
        for s in range(8):
            at = pl.multiple_of(x * 1024 + s * 128, 128)
            out[0, :, pl.ds(at, 128)] = lines[pl.ds(s, 19, stride=8), :]
        return carry

    lax.fori_loop(0, EDGE, plane, 0)


def spread_kernel(planes, slots, old, out):
    def plane(x, carry):
        for slot in range(slots):
            for s in range(8):
                at = pl.multiple_of(x * 1024 + s * 128, 128)
                out[x, pl.ds(slot * 152 + s, 19, stride=8), :] = old[slot, :, pl.ds(at, 128)]
        return carry

    lax.fori_loop(0, planes, plane, 0)


def exchange_kernel(layers, xy, zu, zd, rxy, rb, ra, send_sem, recv_sem):
    me = lax.axis_index("blocks")
    layer, place = me // 4, me % 4
    above, below = layer + 1 < layers, layer > 0
    barrier = pltpu.get_barrier_semaphore()

    def greet(first, k):
        pl.semaphore_signal(
            barrier, inc=1, device_id=(first * 4 + (place + k) % 4,), device_id_type=MESH
        )

    for k in range(1, 4):
        greet(layer, k)

    @pl.when(above)
    def _():
        for k in range(4):
            greet(layer + 1, k)

    @pl.when(below)
    def _():
        for k in range(4):
            greet(layer - 1, k)

    peers = 3 + 4 * above.astype(jnp.int32) + 4 * below.astype(jnp.int32)
    pl.semaphore_wait(barrier, peers)

    def copy(source, target, spot, number, first, k):
        return pltpu.make_async_remote_copy(
            src_ref=source,
            dst_ref=target.at[spot],
            send_sem=send_sem.at[number],
            recv_sem=recv_sem.at[number],
            device_id=(first * 4 + (place + k) % 4,),
            device_id_type=MESH,
        )

    @pl.when(above)
    def _():
        for k in range(4):
            copy(zu, rb, place, 3 + k, layer + 1, k).start()

    @pl.when(below)
    def _():
        for k in range(4):
            copy(zd, ra, place, 7 + k, layer - 1, k).start()

    for k in range(1, 4):
        copy(xy, rxy, place, k - 1, layer, k).start()
    for k in range(1, 4):
        copy(xy, rxy, (place + 4 - k) % 4, k - 1, layer, k).wait_recv()

    @pl.when(below)
    def _():
        for k in range(4):
            copy(zu, rb, (place + 4 - k) % 4, 3 + k, layer - 1, k).wait_recv()

    @pl.when(above)
    def _():
        for k in range(4):
            copy(zd, ra, (place + 4 - k) % 4, 7 + k, layer + 1, k).wait_recv()

    @pl.when(above)
    def _():
        for k in range(4):
            copy(zu, rb, place, 3 + k, layer + 1, k).wait_send()

    @pl.when(below)
    def _():
        for k in range(4):
            copy(zd, ra, place, 7 + k, layer - 1, k).wait_send()

    for k in range(1, 4):
        copy(xy, rxy, place, k - 1, layer, k).wait_send()


VMEM = pl.BlockSpec(memory_space=pltpu.VMEM)
SMEM = pl.BlockSpec(memory_space=pltpu.SMEM)
FACE = jax.ShapeDtypeStruct((5, 8, 128), jnp.float32)
FACES = jax.ShapeDtypeStruct((10, 8, 128), jnp.float32)
STATE = jax.ShapeDtypeStruct((EDGE, 19, 8, 128), jnp.float32)
ROWS = pltpu.VMEM((5, EDGE, 128), jnp.float32)
GHOSTS = pltpu.VMEM((5, EDGE + 8, 128), jnp.float32)
LIMIT = pltpu.CompilerParams(vmem_limit_bytes=40 * 2**20)


def exchange(xy, zu, zd):
    layers = lax.axis_size("blocks") // 4
    return pl.pallas_call(
        functools.partial(exchange_kernel, layers),
        out_shape=[
            jax.ShapeDtypeStruct((4, 10, 8, 128), jnp.float32),
            jax.ShapeDtypeStruct((4, 5, 8, 128), jnp.float32),
            jax.ShapeDtypeStruct((4, 5, 8, 128), jnp.float32),
        ],
        in_specs=[VMEM] * 3,
        out_specs=[VMEM] * 3,
        scratch_shapes=[pltpu.SemaphoreType.DMA((11,)), pltpu.SemaphoreType.DMA((11,))],
        compiler_params=pltpu.CompilerParams(collective_id=0, has_side_effects=True),
    )(xy, zu, zd)


def migrate(old_pdfs, old_slot):
    peers = lax.axis_size("blocks")
    slots = old_pdfs.shape[0]
    blocks = old_slot.shape[0]
    planes = 4
    tiles = pl.pallas_call(
        functools.partial(spread_kernel, planes, slots),
        grid=(EDGE // planes,),
        out_shape=jax.ShapeDtypeStruct((EDGE, slots * 152, 128), jnp.float32),
        in_specs=[pl.BlockSpec((slots, 19, planes * 1024), lambda g: (0, 0, g))],
        out_specs=pl.BlockSpec((planes, slots * 152, 128), lambda g: (g, 0, 0)),
        compiler_params=LIMIT,
    )(old_pdfs)
    parts = peers // EDGE
    rows = 8 // parts
    if parts > 1:
        tiles = tiles.reshape(EDGE, slots * 19, parts, rows, 128).transpose(0, 2, 1, 3, 4)
        tiles = tiles.reshape(peers, slots * 19 * rows, 128)
    spread = lax.all_to_all(tiles, "blocks", split_axis=0, concat_axis=0, tiled=True)
    spread = spread.reshape(peers * slots, 19 * rows, 128)
    ordered = spread.at[old_slot].get(mode="promise_in_bounds")
    arrived = lax.all_to_all(ordered, "blocks", split_axis=0, concat_axis=0, tiled=True)
    if parts > 1:
        arrived = arrived.reshape(EDGE, parts, 19, rows, 128).transpose(0, 2, 1, 3, 4)
    return arrived.reshape(EDGE, 19, 8, 128)


def per_device(old_pdfs, old_slot, neighbours, cell_flags):
    state = migrate(old_pdfs, old_slot)
    flags = cell_flags.reshape(EDGE, 8, 128)
    c, xy, zu, zd = pl.pallas_call(
        first_kernel,
        out_shape=[STATE, FACES, FACE, FACE],
        in_specs=[SMEM, VMEM],
        out_specs=[VMEM] * 4,
        scratch_shapes=[ROWS],
        compiler_params=LIMIT,
    )(neighbours, state)
    for _ in range(STEPS - 1):
        rxy, rb, ra = exchange(xy, zu, zd)
        c, xy, zu, zd = pl.pallas_call(
            middle_kernel,
            out_shape=[STATE, FACES, FACE, FACE],
            in_specs=[SMEM] + [VMEM] * 5,
            out_specs=[VMEM] * 4,
            scratch_shapes=[ROWS, GHOSTS],
            compiler_params=LIMIT,
        )(neighbours, flags, c, rxy, rb, ra)
    rxy, rb, ra = exchange(xy, zu, zd)
    return pl.pallas_call(
        last_kernel,
        out_shape=jax.ShapeDtypeStruct((1, 19, EDGE * EDGE * EDGE), jnp.float32),
        in_specs=[SMEM] + [VMEM] * 5,
        out_specs=VMEM,
        scratch_shapes=[GHOSTS, pltpu.VMEM((152, 128), jnp.float32)],
        compiler_params=LIMIT,
    )(neighbours, flags, c, rxy, rb, ra)


def solution(mesh):
    in_specs = (P("blocks", None, None), P(), P("blocks", None), P("blocks", None))
    out_specs = P("blocks", None, None)
    return jax.shard_map(
        per_device, mesh=mesh, in_specs=in_specs, out_specs=out_specs, check_vma=False
    )
```

time: 2010 us -> 245 us (0.12); the launches traced: 1980 us -> 245 us
  local copies, waits for them, and re-layouts: 1160 us -> 26.8 us
  other arithmetic: 434 us -> 0.01 us
  starting transfers between devices: 166 us -> 7.41 us
  waiting for transfers between devices: 174 us -> 111 us
  blocking collectives: 0 us -> 61.6 us
  Pallas kernels: 0 us -> 37.7 us
  matrix products: 25.6 us -> 0 us
    scatter x283 -> x0, local copies, waits for them, and re-layouts: 695 us -> none
    scatter x120 -> x0, other arithmetic: 313 us -> none
    unnamed x237 -> x37, local copies, waits for them, and re-layouts: 202 us -> 19.7 us
    ppermute x56 -> x0, starting transfers between devices: 154 us -> none  [from_behind(): return lax.ppermute(shard, axis, pairs)]
    another operation x108 -> x0, local copies, waits for them, and re-layouts: 117 us -> none  [the longest x40 64.9 us: propagate(): return jnp.stack(results, axis=1)]
    gather x17 -> x1, local copies, waits for them, and re-layouts: 67.6 us -> 3.12 us  [migrate(): ordered = spread.at[old_slot].get(mode='promise_in_bounds')]
    all_to_all x0 -> x1, blocking collectives: none -> 61.6 us  [migrate(): lax.all_to_all(ordered, 'blocks', split_axis=0, concat_axis=0, tiled=True)]
    all_to_all x1 -> x0, other arithmetic: 53.5 us -> none  [per_device(): lax.all_to_all(old_pdfs, 'blocks', split_axis=2, concat_axis=0, tiled=True)]
  transfers between devices with their start and end apart: 58 -> 1, of which waited for: 10 -> 1; matrix products, arithmetic and copies ran while one was open for 5% -> 0% of each run, Pallas kernels for 0% -> 0%
where the time goes in v1:
time: 245 us
  waiting for transfers between devices  111 us (45%)
  blocking collectives  61.6 us (25%)
  Pallas kernels  37.7 us (15%)
  local copies, waits for them, and re-layouts  26.8 us (11%)
  starting transfers between devices  7.41 us (3%)
    all_to_all x1, waiting for transfers between devices, migrate(): lax.all_to_all(tiles, 'blocks', split_axis=0, concat_axis=0, tiled=True)  111 us
    all_to_all x1, blocking collectives, migrate(): lax.all_to_all(ordered, 'blocks', split_axis=0, concat_axis=0, tiled=True)  61.6 us
    unnamed x37, local copies, waits for them, and re-layouts  19.7 us
    pallas_call x2, Pallas kernels, exchange(): pl.pallas_call(functools.partial(exchange_kernel, layers), out_shape=[jax...  16.8 us
    pallas_call x1, Pallas kernels, per_device(): pl.pallas_call(middle_kernel, out_shape=[STATE, FACES, FACE, FACE], in_sp...  8.99 us
    all_to_all x1, starting transfers between devices, migrate(): lax.all_to_all(tiles, 'blocks', split_axis=0, concat_axis=0, tiled=True)  7.41 us
    pallas_call x1, Pallas kernels, per_device(): pl.pallas_call(last_kernel, out_shape=jax.ShapeDtypeStruct((1, 19, EDGE *...  5.86 us
  transfers between devices with their start and end apart: 1, of which 1 were waited for; matrix products, arithmetic and copies ran while one was open for 0% of the time, Pallas kernels for 0%

profile of v1, /device:TPU:0, one launch (start us, length us, event | category | flops | bytes accessed | tf_op | source)
XLA Modules:
  0.0 244.6 jit_solution(15171401668381996068)
XLA Ops:
  0.0 5.3 %copy.5.old = f32[2,19,32768]{2,1,0:T(8,128)S(1)} copy(f32[2,19,32768]{2,0,1:T(2,128)} %param.4) | data formatting | bytes 9961472 | tf_op args[0]
  5.3 1.8 shard_map.46
  7.1 0.0 copy-start
  7.1 2.2 copy-done
  9.4 0.0 copy-start.17
  9.4 7.4 %all-to-all-start = ((f32[32,304,128]{2,1,0:T(8,128)}), f32[32,304,128]{2,1,0:T(8,128)}, u32[]{:S(2)}, u32[]{:S(2)}) async-start(f32[32,304,128]{2,1,0:T(8,128)} %copy-done), calls=%async_computation | async-start | bytes 9961472 | tf_op jit(solution)/shard_map/all_to_all | solution.py:516
  16.8 0.0 copy-done.17
  16.8 111.0 %all-to-all-done = f32[32,304,128]{2,1,0:T(8,128)} async-done(((f32[32,304,128]{2,1,0:T(8,128)}), f32[32,304,128]{2,1,0:T(8,128)}, u32[]{:S(2)}, u32[]{:S(2)}) %all-to-all-start) | async-done | bytes 4980768 | tf_op jit(solution)/shard_map/all_to_all | solution.py:516
  127.8 3.1 %gather_fusion = f32[32,152,128]{2,1,0:T(8,128)S(1)} fusion(f32[64,152,128]{2,1,0:T(8,128)} %bitcast.1, s32[1024]{0:T(1024)S(1)} %pad_clamp_fusion), kind=kCustom, calls=%fused_computation | custom fusion | bytes 4980864 | tf_op jit(solution)/shard_map/gather | solution.py:518
  130.9 0.0 copy-start.16
  130.9 61.6 %all_to_all.10 = f32[32,152,128]{2,1,0:T(8,128)S(1)} all-to-all(f32[32,152,128]{2,1,0:T(8,128)S(1)} %gather_fusion), channel_id=1, replica_groups=mesh['blocks'=32] {'blocks'}, dimensions={0} | all-to-all | bytes 4980736 | tf_op jit(solution)/shard_map/all_to_all | solution.py:519
  192.5 0.0 copy-start.3
  192.5 0.0 copy-done.16
  192.5 4.3 %shard_map.47 = (f32[32,19,8,128]{3,2,1,0:T(8,128)S(1)}, f32[10,8,128]{2,1,0:T(8,128)S(1)}, f32[5,8,128]{2,1,0:T(8,128)S(1)}, f32[5,8,128]{2,1,0:T(8,128)S(1)}) custom-call(s32[1,18]{1,0:T(1,128)S(1)} %copy-done.16, f32[32,19,8,128]{3,2,1,0:T(8,128)S(1)} %bitcast.3), custom_call_target="tpu_custom_call" | custom-call | tf_op jit(solution)/shard_map/pallas_call | solution.py:528
  196.8 0.0 copy-start.11
  196.8 0.6 copy-done.11
  197.4 0.0 copy-start.14
  197.4 0.6 copy-done.14
  198.0 0.0 copy-start.15
  198.0 0.6 copy-done.15
  198.6 8.3 %shard_map.48 = (f32[4,10,8,128]{3,2,1,0:T(8,128)}, f32[4,5,8,128]{3,2,1,0:T(8,128)}, f32[4,5,8,128]{3,2,1,0:T(8,128)}) custom-call(f32[10,8,128]{2,1,0:T(8,128)} %copy-done.11, f32[5,8,128]{2,1,0:T(8,128)} %copy-done.14, f32[5,8,128]{2,1,0:T(8,128)} %copy-done.15), custom_call_target="tpu_custom_call" | custom-call | tf_op jit(solution)/shard_map/pallas_call | solution.py:484
  206.9 0.0 copy-done.3
  206.9 0.0 copy-start.4
  206.9 0.9 copy-done.4
  207.8 0.0 copy-start.6
  207.8 0.9 copy-done.6
  208.7 0.0 copy-start.7
  208.7 0.9 copy-done.7
  209.6 9.0 %shard_map.49 = (f32[32,19,8,128]{3,2,1,0:T(8,128)S(1)}, f32[10,8,128]{2,1,0:T(8,128)S(1)}, f32[5,8,128]{2,1,0:T(8,128)S(1)}, f32[5,8,128]{2,1,0:T(8,128)S(1)}) custom-call(s32[1,18]{1,0:T(1,128)S(1)} %copy-done.16, s32[32,8,128]{2,1,0:T(8,128)S(1)} %bitcast.4, f32[32,19,8,128]{3,2,1,0:T(8,128)S(1)} %get-tuple-element.19.c_in, ...), custom_call_target="tpu_custom_call" | custom-call | tf_op jit(solution)/shard_map/pallas_call | solution.py:538
  218.6 0.0 copy-start.1
  218.6 1.4 copy-done.1
  220.1 0.0 copy-start.10
  220.1 0.6 copy-done.10
  220.7 0.0 copy-start.12
  220.7 0.6 copy-done.12
  221.3 0.0 copy-start.13
  221.3 0.6 copy-done.13
  221.9 8.5 %shard_map.50 = (f32[4,10,8,128]{3,2,1,0:T(8,128)}, f32[4,5,8,128]{3,2,1,0:T(8,128)}, f32[4,5,8,128]{3,2,1,0:T(8,128)}) custom-call(f32[10,8,128]{2,1,0:T(8,128)} %copy-done.10, f32[5,8,128]{2,1,0:T(8,128)} %copy-done.12, f32[5,8,128]{2,1,0:T(8,128)} %copy-done.13), custom_call_target="tpu_custom_call" | custom-call | tf_op jit(solution)/shard_map/pallas_call | solution.py:484
  230.4 0.0 copy-start.2
  230.4 1.7 copy-done.2
  232.1 0.0 copy-start.5
  232.1 0.9 copy-done.5
  233.0 0.0 copy-start.8
  233.0 0.9 copy-done.8
  233.9 0.0 copy-start.9
  233.9 0.9 copy-done.9
  234.8 5.9 %shard_map.51 = f32[1,19,32768]{2,1,0:T(8,128)S(1)} custom-call(s32[1,18]{1,0:T(1,128)S(1)} %copy-done.16, s32[32,8,128]{2,1,0:T(8,128)S(1)} %bitcast.5, f32[32,19,8,128]{3,2,1,0:T(8,128)S(1)} %copy-done.2, f32[4,10,8,128]{3,2,1,0:T(8,128)S(1)} %copy-done.5, f32[4,5,8,128]{3,2,1,0:T(8,128)S(1)} %copy-done.8, f32[4,5,8,128]{3,2,1,0:T(8,128)S(1)} %copy-done.9), custom_call_target="tpu_custom_call" | custom-call | tf_op jit(solution)/shard_map/pallas_call | solution.py:547
  240.6 4.0 %copy.6 = f32[1,19,32768]{2,0,1:T(1,128)} copy(f32[1,19,32768]{2,1,0:T(8,128)S(1)} %shard_map.51) | data formatting | bytes 4980736 | tf_op jit(solution)/shard_map/pallas_call | solution.py:547
  (2 shorter events, 0.0 us)
Async XLA Ops:
  7.1 2.3 copy-start
  9.4 7.4 %copy-start.17 = (s32[32]{0:T(128)S(1)}, s32[32]{0:T(128)}, u32[]{:S(2)}) copy-start(s32[32]{0:T(128)} %param.5) | copy-start | bytes 388
  9.4 118.4 %all-to-all-start = ((f32[32,304,128]{2,1,0:T(8,128)}), f32[32,304,128]{2,1,0:T(8,128)}, u32[]{:S(2)}, u32[]{:S(2)}) async-start(f32[32,304,128]{2,1,0:T(8,128)} %copy-done), calls=%async_computation | async-start | bytes 9961472 | tf_op jit(solution)/shard_map/all_to_all | solution.py:516
  130.9 61.6 %copy-start.16 = (s32[1,18]{1,0:T(1,128)S(1)}, s32[1,18]{1,0:T(1,128)}, u32[]{:S(2)}) copy-start(s32[1,18]{1,0:T(1,128)} %nbr.5) | copy-start | bytes 220
  192.5 14.4 %copy-start.3 = (s32[1,32768]{1,0:T(1,128)S(1)}, s32[1,32768]{1,0:T(1,128)}, u32[]{:S(2)}) copy-start(s32[1,32768]{1,0:T(1,128)} %param.7) | copy-start | bytes 393220
  196.8 0.6 copy-start.11
  197.4 0.6 copy-start.14
  198.0 0.6 copy-start.15
  206.9 0.9 copy-start.4
  207.8 0.9 copy-start.6
  208.7 0.9 copy-start.7
  218.6 1.5 copy-start.1
  220.1 0.6 copy-start.10
  220.7 0.6 copy-start.12
  221.3 0.6 copy-start.13
  230.4 1.7 copy-start.2
  232.1 0.9 copy-start.5
  233.0 0.9 copy-start.8
  233.9 0.9 copy-start.9

commit v2 on v1

--- a/solution.py
+++ b/solution.py
@@ -495,6 +495,159 @@
     )(xy, zu, zd)
 
 
+CHUNKS = ((0, 0, 10), (1, 0, 10), (0, 10, 19), (1, 10, 19))
+CAPACITIES = (10, 12, 16)
+
+
+def migrate_kernel(room, plan, tiles, out, *scratch):
+    parts = len(CHUNKS)
+    held, wanted, given, sorted_ = (scratch[parts * n : parts * n + parts] for n in range(4))
+    own_sem, send_one, recv_one, send_two, recv_two, send_three, recv_three = scratch[4 * parts :]
+    me = lax.axis_index("blocks")
+    half, place = me // 16, me % 16
+    partner = (1 - half) * 16 + place
+
+    def peer(d):
+        return (place + d) % 16
+
+    def device(d):
+        return (half * 16 + peer(d),)
+
+    barrier = pltpu.get_barrier_semaphore()
+
+    def greet(d, carry):
+        pl.semaphore_signal(barrier, inc=1, device_id=device(d), device_id_type=MESH)
+        return carry
+
+    lax.fori_loop(1, 16, greet, 0)
+    pl.semaphore_signal(barrier, inc=1, device_id=(partner,), device_id_type=MESH)
+    pl.semaphore_wait(barrier, 16)
+
+    def spread(k, d, owner):
+        plane, low, high = CHUNKS[k]
+        return pltpu.make_async_remote_copy(
+            src_ref=tiles.at[2 * peer(d) + plane, :, low:high],
+            dst_ref=held[k].at[pl.ds(2 * owner, 2)],
+            send_sem=send_one.at[k, d],
+            recv_sem=recv_one.at[k, d],
+            device_id=device(d),
+            device_id_type=MESH,
+        )
+
+    def keep(k):
+        plane, low, high = CHUNKS[k]
+        return pltpu.make_async_copy(
+            tiles.at[2 * place + plane, :, low:high], held[k].at[pl.ds(2 * place, 2)], own_sem.at[k]
+        )
+
+    def swap(k):
+        return pltpu.make_async_remote_copy(
+            src_ref=wanted[k],
+            dst_ref=given[k],
+            send_sem=send_two.at[k],
+            recv_sem=recv_two.at[k],
+            device_id=(partner,),
+            device_id_type=MESH,
+        )
+
+    def hand(k, d, owner):
+        plane, low, high = CHUNKS[k]
+        return pltpu.make_async_remote_copy(
+            src_ref=sorted_[k].at[peer(d)],
+            dst_ref=out.at[2 * owner + plane, low:high],
+            send_sem=send_three.at[k, d],
+            recv_sem=recv_three.at[k, d],
+            device_id=device(d),
+            device_id_type=MESH,
+        )
+
+    def each(body):
+        def step(d, carry):
+            body(d)
+            return carry
+
+        lax.fori_loop(1, 16, step, 0)
+
+    def deliver(k):
+        plane, low, high = CHUNKS[k]
+        swap(k).wait_recv()
+
+        def choose(b, carry):
+            near, far = held[k][plan[2, b]], given[k][plan[3, b]]
+            sorted_[k][b] = jnp.where(plan[1, b] > 0, near, far)
+            return carry
+
+        lax.fori_loop(0, 16, choose, 0)
+        each(lambda d: hand(k, d, place).start())
+        out[2 * place + plane, low:high] = sorted_[k][place]
+
+    for k in range(parts):
+        keep(k).start()
+        each(lambda d: spread(k, d, place).start())
+    for k in range(parts):
+        keep(k).wait()
+        each(lambda d: spread(k, d, peer(16 - d)).wait_recv())
+
+        def pick(e, carry):
+            wanted[k][e] = held[k][plan[0, e]]
+            return carry
+
+        lax.fori_loop(0, room, pick, 0)
+        swap(k).start()
+        if k > 0:
+            deliver(k - 1)
+    deliver(parts - 1)
+    for k in range(parts):
+        each(lambda d: hand(k, d, peer(16 - d)).wait_recv())
+    for k in range(parts):
+        each(lambda d: spread(k, d, place).wait_send())
+        swap(k).wait_send()
+        each(lambda d: hand(k, d, place).wait_send())
+
+
+def migrate_with(room, number, plan, tiles):
+    parts = len(CHUNKS)
+
+    def buffers(count):
+        return [pltpu.VMEM((count, high - low, 8, 128), jnp.float32) for _, low, high in CHUNKS]
+
+    dma = pltpu.SemaphoreType.DMA
+    return pl.pallas_call(
+        functools.partial(migrate_kernel, room),
+        out_shape=STATE,
+        in_specs=[SMEM, VMEM],
+        out_specs=VMEM,
+        scratch_shapes=buffers(32)
+        + buffers(room)
+        + buffers(room)
+        + buffers(16)
+        + [dma((parts,)), dma((parts, 16)), dma((parts, 16)), dma((parts,)), dma((parts,))]
+        + [dma((parts, 16)), dma((parts, 16))],
+        compiler_params=pltpu.CompilerParams(
+            collective_id=number, has_side_effects=True, vmem_limit_bytes=40 * 2**20
+        ),
+    )(plan, tiles)
+
+
+def migration_plan(old_slot):
+    half = lax.axis_index("blocks") // 16
+    block = jnp.arange(32, dtype=jnp.int32)
+    from_half, to_half = old_slot // 32, block // 16
+    crosses = from_half != to_half
+    same = (to_half[None, :] == to_half[:, None]) & (block[None, :] < block[:, None])
+    rank = jnp.sum((same & crosses[None, :]).astype(jnp.int32), axis=1)
+    leaves = crosses & (from_half == half)
+    entry = jnp.arange(16, dtype=jnp.int32)
+    chosen = leaves[None, :] & (rank[None, :] == entry[:, None])
+    local = old_slot % 32
+    wanted = jnp.sum(jnp.where(chosen, local[None, :], 0), axis=1)
+    mine = lax.dynamic_slice_in_dim(jnp.stack([1 - crosses.astype(jnp.int32), local, rank]), half * 16, 16, 1)
+    stays = mine[0]
+    plan = jnp.stack([wanted, stays, mine[1] * stays, mine[2] * (1 - stays)])
+    counts = [jnp.sum((crosses & (to_half == h)).astype(jnp.int32)) for h in range(2)]
+    return plan, jnp.maximum(counts[0], counts[1])
+
+
 def migrate(old_pdfs, old_slot):
     peers = lax.axis_size("blocks")
     slots = old_pdfs.shape[0]
@@ -508,6 +661,15 @@
         out_specs=pl.BlockSpec((planes, slots * 152, 128), lambda g: (g, 0, 0)),
         compiler_params=LIMIT,
     )(old_pdfs)
+    if peers == EDGE and slots == 2:
+        plan, most = migration_plan(old_slot)
+        branch = sum((most > room).astype(jnp.int32) for room in CAPACITIES[:-1])
+        tiles = tiles.reshape(EDGE, slots, 19, 8, 128)
+        calls = [
+            functools.partial(migrate_with, room, 1 + number)
+            for number, room in enumerate(CAPACITIES)
+        ]
+        return lax.switch(branch, calls, plan, tiles)
     parts = peers // EDGE
     rows = 8 // parts
     if parts > 1:

time: 245 us -> 199 us (0.81)
  Pallas kernels: 37.7 us -> 171 us
  waiting for transfers between devices: 111 us -> 0 us
  blocking collectives: 61.6 us -> 0 us
  starting transfers between devices: 7.41 us -> 0 us
  local copies, waits for them, and re-layouts: 26.8 us -> 21.5 us
  other arithmetic: 0.01 us -> 3.04 us
    pallas_call x0 -> x1, Pallas kernels: none -> 130 us  [migrate_with(): pl.pallas_call(functools.partial(migrate_kernel, room), out_shape=STATE,...]
    all_to_all x1 -> x0, waiting for transfers between devices: 111 us -> none  [migrate(): lax.all_to_all(tiles, 'blocks', split_axis=0, concat_axis=0, tiled=True)]
    all_to_all x1 -> x0, blocking collectives: 61.6 us -> none  [migrate(): lax.all_to_all(ordered, 'blocks', split_axis=0, concat_axis=0, tiled=True)]
    all_to_all x1 -> x0, starting transfers between devices: 7.41 us -> none  [migrate(): lax.all_to_all(tiles, 'blocks', split_axis=0, concat_axis=0, tiled=True)]
    gather x1 -> x0, local copies, waits for them, and re-layouts: 3.12 us -> none  [migrate(): ordered = spread.at[old_slot].get(mode='promise_in_bounds')]
    unnamed x37 -> x33, local copies, waits for them, and re-layouts: 19.7 us -> 17.4 us
  transfers between devices with their start and end apart: 1 -> 0, of which waited for: 1 -> 0; matrix products, arithmetic and copies ran while one was open for 0% -> 0% of each run, Pallas kernels for 0% -> 0%
where the time goes in v2:
time: 199 us; the launch traced here: 197 us
  Pallas kernels  171 us (86%)
  local copies, waits for them, and re-layouts  21.5 us (11%)
  other arithmetic  3.04 us (2%)
    pallas_call x1, Pallas kernels, migrate_with(): pl.pallas_call(functools.partial(migrate_kernel, room), out_shape=STATE,...  130 us
    pallas_call x2, Pallas kernels, exchange(): pl.pallas_call(functools.partial(exchange_kernel, layers), out_shape=[jax...  19.1 us
    unnamed x33, local copies, waits for them, and re-layouts  17.4 us
    pallas_call x1, Pallas kernels, per_device(): pl.pallas_call(middle_kernel, out_shape=[STATE, FACES, FACE, FACE], in_sp...  8.99 us
    pallas_call x1, Pallas kernels, per_device(): pl.pallas_call(last_kernel, out_shape=jax.ShapeDtypeStruct((1, 19, EDGE *...  5.86 us
    pallas_call x1, Pallas kernels, per_device(): pl.pallas_call(first_kernel, out_shape=[STATE, FACES, FACE, FACE], in_spe...  5.51 us
    pallas_call x1, local copies, waits for them, and re-layouts, per_device(): pl.pallas_call(last_kernel, out_shape=jax.ShapeDtypeStruct((1, 19, EDGE *...  4.01 us

profile of v2, /device:TPU:0, one launch (start us, length us, event | category | flops | bytes accessed | tf_op | source)
XLA Modules:
  0.0 197.0 jit_solution(8445746991493378341)
XLA Ops:
  0.0 0.7 fusion.7
  0.7 0.7 and_select_fusion
  1.3 0.7 compare_and_fusion
  2.0 0.2 convert_reduce_fusion
  2.2 0.1 select_reduce_fusion
  2.3 0.7 fusion.4
  4.3 0.1 constant_dynamic-slice_fusion
  4.4 5.3 %copy.7.old = f32[2,19,32768]{2,1,0:T(8,128)S(1)} copy(f32[2,19,32768]{2,0,1:T(2,128)} %param.7) | data formatting | bytes 9961472 | tf_op args[0]
  9.7 1.8 shard_map.46
  11.5 0.0 copy-start.15
  11.5 129.8 %conditional.1 = (f32[32,19,8,128]{3,2,1,0:T(8,128)}) conditional(s32[]{:T(128)} %clamp.3, (s32[4,16]{1,0:T(4,128)S(1)}, f32[32,2,19,8,128]{4,3,2,1,0:T(8,128)S(1)}) %tuple.23, (s32[4,16]{1,0:T(4,128)S(1)}, f32[32,2,19,8,128]{4,3,2,1,0:T(8,128)S(1)}) %tuple.24, (s32[4,16]{1,0:T(4,128)S(1)}, ...), branch_computations={%region_4.5_spmd, %region_5.6_spmd, %region_6.7_spmd} | conditional | bytes 8 | solution.py:672
  11.5 129.8 %branch_0_fun.1 = f32[32,19,8,128]{3,2,1,0:T(8,128)} custom-call(s32[4,16]{1,0:T(4,128)S(1)} %get-tuple-element.20.plan, f32[32,2,19,8,128]{4,3,2,1,0:T(8,128)S(1)} %get-tuple-element.22.tiles), custom_call_target="tpu_custom_call" | custom-call | tf_op jit(solution)/shard_map/cond/branch_0_fun/pallas_call | solution.py:615
  141.3 0.0 copy-start.2
  141.3 0.0 copy-done.15
  141.3 5.5 %shard_map.47 = (f32[32,19,8,128]{3,2,1,0:T(8,128)S(1)}, f32[10,8,128]{2,1,0:T(8,128)S(1)}, f32[5,8,128]{2,1,0:T(8,128)S(1)}, f32[5,8,128]{2,1,0:T(8,128)S(1)}) custom-call(s32[1,18]{1,0:T(1,128)S(1)} %copy-done.15, f32[32,19,8,128]{3,2,1,0:T(8,128)} %get-tuple-element.63.f), custom_call_target="tpu_custom_call" | custom-call | tf_op jit(solution)/shard_map/pallas_call | solution.py:690
  146.9 0.0 copy-start.10
  146.9 0.6 copy-done.10
  147.5 0.0 copy-start.13
  147.5 0.6 copy-done.13
  148.1 0.0 copy-start.14
  148.1 0.6 copy-done.14
  148.7 10.0 %shard_map.48 = (f32[4,10,8,128]{3,2,1,0:T(8,128)}, f32[4,5,8,128]{3,2,1,0:T(8,128)}, f32[4,5,8,128]{3,2,1,0:T(8,128)}) custom-call(f32[10,8,128]{2,1,0:T(8,128)} %copy-done.10, f32[5,8,128]{2,1,0:T(8,128)} %copy-done.13, f32[5,8,128]{2,1,0:T(8,128)} %copy-done.14), custom_call_target="tpu_custom_call" | custom-call | tf_op jit(solution)/shard_map/pallas_call | solution.py:484
  158.7 0.0 copy-done.2
  158.7 0.0 copy-start.3
  158.7 0.9 copy-done.3
  159.6 0.0 copy-start.5
  159.6 0.9 copy-done.5
  160.5 0.0 copy-start.6
  160.5 0.9 copy-done.6
  161.4 9.0 %shard_map.49 = (f32[32,19,8,128]{3,2,1,0:T(8,128)S(1)}, f32[10,8,128]{2,1,0:T(8,128)S(1)}, f32[5,8,128]{2,1,0:T(8,128)S(1)}, f32[5,8,128]{2,1,0:T(8,128)S(1)}) custom-call(s32[1,18]{1,0:T(1,128)S(1)} %copy-done.15, s32[32,8,128]{2,1,0:T(8,128)S(1)} %bitcast.8, f32[32,19,8,128]{3,2,1,0:T(8,128)S(1)} %get-tuple-element.41.c_in, ...), custom_call_target="tpu_custom_call" | custom-call | tf_op jit(solution)/shard_map/pallas_call | solution.py:700
  170.4 0.0 copy-start
  170.4 1.4 copy-done
  171.9 0.0 copy-start.9
  171.9 0.6 copy-done.9
  172.5 0.0 copy-start.11
  172.5 0.6 copy-done.11
  173.0 0.0 copy-start.12
  173.0 0.6 copy-done.12
  173.6 9.1 %shard_map.50 = (f32[4,10,8,128]{3,2,1,0:T(8,128)}, f32[4,5,8,128]{3,2,1,0:T(8,128)}, f32[4,5,8,128]{3,2,1,0:T(8,128)}) custom-call(f32[10,8,128]{2,1,0:T(8,128)} %copy-done.9, f32[5,8,128]{2,1,0:T(8,128)} %copy-done.11, f32[5,8,128]{2,1,0:T(8,128)} %copy-done.12), custom_call_target="tpu_custom_call" | custom-call | tf_op jit(solution)/shard_map/pallas_call | solution.py:484
  182.8 0.0 copy-start.1
  182.8 1.7 copy-done.1
  184.5 0.0 copy-start.4
  184.5 0.9 copy-done.4
  185.4 0.9 copy-done.7
  186.3 0.0 copy-start.8
  186.3 0.9 copy-done.8
  187.2 5.9 %shard_map.51 = f32[1,19,32768]{2,1,0:T(8,128)S(1)} custom-call(s32[1,18]{1,0:T(1,128)S(1)} %copy-done.15, s32[32,8,128]{2,1,0:T(8,128)S(1)} %bitcast.9, f32[32,19,8,128]{3,2,1,0:T(8,128)S(1)} %copy-done.1, f32[4,10,8,128]{3,2,1,0:T(8,128)S(1)} %copy-done.4, f32[4,5,8,128]{3,2,1,0:T(8,128)S(1)} %copy-done.7, f32[4,5,8,128]{3,2,1,0:T(8,128)S(1)} %copy-done.8), custom_call_target="tpu_custom_call" | custom-call | tf_op jit(solution)/shard_map/pallas_call | solution.py:709
  193.0 4.0 %copy.8 = f32[1,19,32768]{2,0,1:T(1,128)} copy(f32[1,19,32768]{2,1,0:T(8,128)S(1)} %shard_map.51) | data formatting | bytes 4980736 | tf_op jit(solution)/shard_map/pallas_call | solution.py:709
  (6 shorter events, 0.0 us)
Async XLA Ops:
  11.5 129.8 %copy-start.15 = (s32[1,18]{1,0:T(1,128)S(1)}, s32[1,18]{1,0:T(1,128)}, u32[]{:S(2)}) copy-start(s32[1,18]{1,0:T(1,128)} %nbr.5) | copy-start | bytes 220
  141.3 17.4 %copy-start.2 = (s32[1,32768]{1,0:T(1,128)S(1)}, s32[1,32768]{1,0:T(1,128)}, u32[]{:S(2)}) copy-start(s32[1,32768]{1,0:T(1,128)} %param.10) | copy-start | bytes 393220
  146.9 0.6 copy-start.10
  147.5 0.6 copy-start.13
  148.1 0.6 copy-start.14
  158.7 0.9 copy-start.3
  159.6 0.9 copy-start.5
  160.5 0.9 copy-start.6
  170.4 1.5 copy-start
  171.9 0.6 copy-start.9
  172.5 0.6 copy-start.11
  173.0 0.6 copy-start.12
  182.8 1.7 copy-start.1
  184.5 0.9 copy-start.4
  185.4 0.9 copy-start.7
  186.3 0.9 copy-start.8

commit v3 on v2

--- a/solution.py
+++ b/solution.py
@@ -336,50 +336,51 @@
         xy[5 + k] = packed
 
 
-def first_kernel(nbr, f, c, xy, zu, zd, rows):
-    zu[...] = jnp.zeros_like(zu)
-    zd[...] = jnp.zeros_like(zd)
-
-    def plane(x, carry):
-        collided = collide([f[x, i] for i in range(19)])
+def steps_kernel(layers, nbr, flags, f, out, *scratch):
+    c, messages, landed = scratch[:2], scratch[2 : 2 + 3 * STEPS], scratch[2 + 3 * STEPS : 2 + 6 * STEPS]
+    rows, gy, lines, send_sem, recv_sem = scratch[2 + 6 * STEPS :]
+    wait_entry, send, receive, finish = exchanges(layers, messages, landed, send_sem, recv_sem)
+    for step in range(STEPS):
+        now, before = c[step % 2], c[(step + 1) % 2]
+        xy, zu, zd = messages[3 * step : 3 * step + 3]
+        zu[...] = jnp.zeros_like(zu)
+        zd[...] = jnp.zeros_like(zd)
+        if step > 0:
+            rxy, rb, ra = landed[3 * step - 3 : 3 * step]
+            unpack_ghosts(nbr, rxy, gy)
+
+        def plane(x, carry):
+            if step == 0:
+                old = [f[x, i] for i in range(19)]
+            else:
+                old = pull(x, nbr, before, rxy, rb, ra, flags, gy)
+            collided = collide(old)
+            for i in range(19):
+                now[x, i] = collided[i]
+            note_faces(x, nbr, collided, zu, zd, rows)
+            return carry
+
+        lax.fori_loop(0, EDGE, plane, 0)
+        finish_faces(nbr, now, rows, xy)
+        if step == 0:
+            wait_entry()
+        send(step)
+        receive(step)
+    rxy, rb, ra = landed[3 * STEPS - 3 :]
+    unpack_ghosts(nbr, rxy, gy)
+
+    def last_plane(x, carry):
+        new = pull(x, nbr, now, rxy, rb, ra, flags, gy)
         for i in range(19):
-            c[x, i] = collided[i]
-        note_faces(x, nbr, collided, zu, zd, rows)
-        return carry
-
-    lax.fori_loop(0, EDGE, plane, 0)
-    finish_faces(nbr, c, rows, xy)
-
-
-def middle_kernel(nbr, flags, c_in, rxy, rb, ra, c, xy, zu, zd, rows, gy):
-    zu[...] = jnp.zeros_like(zu)
-    zd[...] = jnp.zeros_like(zd)
-    unpack_ghosts(nbr, rxy, gy)
-
-    def plane(x, carry):
-        collided = collide(pull(x, nbr, c_in, rxy, rb, ra, flags, gy))
-        for i in range(19):
-            c[x, i] = collided[i]
-        note_faces(x, nbr, collided, zu, zd, rows)
-        return carry
-
-    lax.fori_loop(0, EDGE, plane, 0)
-    finish_faces(nbr, c, rows, xy)
-
-
-def last_kernel(nbr, flags, c_in, rxy, rb, ra, out, gy, lines):
-    unpack_ghosts(nbr, rxy, gy)
-
-    def plane(x, carry):
-        f = pull(x, nbr, c_in, rxy, rb, ra, flags, gy)
-        for i in range(19):
-            lines[8 * i : 8 * i + 8, :] = f[i]
+            lines[8 * i : 8 * i + 8, :] = new[i]
         for s in range(8):
             at = pl.multiple_of(x * 1024 + s * 128, 128)
             out[0, :, pl.ds(at, 128)] = lines[pl.ds(s, 19, stride=8), :]
         return carry
 
-    lax.fori_loop(0, EDGE, plane, 0)
+    lax.fori_loop(0, EDGE, last_plane, 0)
+    for step in range(STEPS):
+        finish(step)
 
 
 def spread_kernel(planes, slots, old, out):
@@ -393,7 +394,7 @@
     lax.fori_loop(0, planes, plane, 0)
 
 
-def exchange_kernel(layers, xy, zu, zd, rxy, rb, ra, send_sem, recv_sem):
+def exchanges(layers, messages, landed, send_sem, recv_sem):
     me = lax.axis_index("blocks")
     layer, place = me // 4, me % 4
     above, below = layer + 1 < layers, layer > 0
@@ -417,82 +418,68 @@
         for k in range(4):
             greet(layer - 1, k)
 
-    peers = 3 + 4 * above.astype(jnp.int32) + 4 * below.astype(jnp.int32)
-    pl.semaphore_wait(barrier, peers)
-
-    def copy(source, target, spot, number, first, k):
+    def wait_entry():
+        peers = 3 + 4 * above.astype(jnp.int32) + 4 * below.astype(jnp.int32)
+        pl.semaphore_wait(barrier, peers)
+
+    def copy(step, group, spot, first, k):
         return pltpu.make_async_remote_copy(
-            src_ref=source,
-            dst_ref=target.at[spot],
-            send_sem=send_sem.at[number],
-            recv_sem=recv_sem.at[number],
+            src_ref=messages[3 * step + group],
+            dst_ref=landed[3 * step + group].at[spot],
+            send_sem=send_sem.at[step, 4 * group + k],
+            recv_sem=recv_sem.at[step, 4 * group + k],
             device_id=(first * 4 + (place + k) % 4,),
             device_id_type=MESH,
         )
 
-    @pl.when(above)
-    def _():
-        for k in range(4):
-            copy(zu, rb, place, 3 + k, layer + 1, k).start()
-
-    @pl.when(below)
-    def _():
-        for k in range(4):
-            copy(zd, ra, place, 7 + k, layer - 1, k).start()
-
-    for k in range(1, 4):
-        copy(xy, rxy, place, k - 1, layer, k).start()
-    for k in range(1, 4):
-        copy(xy, rxy, (place + 4 - k) % 4, k - 1, layer, k).wait_recv()
-
-    @pl.when(below)
-    def _():
-        for k in range(4):
-            copy(zu, rb, (place + 4 - k) % 4, 3 + k, layer - 1, k).wait_recv()
-
-    @pl.when(above)
-    def _():
-        for k in range(4):
-            copy(zd, ra, (place + 4 - k) % 4, 7 + k, layer + 1, k).wait_recv()
-
-    @pl.when(above)
-    def _():
-        for k in range(4):
-            copy(zu, rb, place, 3 + k, layer + 1, k).wait_send()
-
-    @pl.when(below)
-    def _():
-        for k in range(4):
-            copy(zd, ra, place, 7 + k, layer - 1, k).wait_send()
-
-    for k in range(1, 4):
-        copy(xy, rxy, place, k - 1, layer, k).wait_send()
+    def send(step):
+        @pl.when(above)
+        def _():
+            for k in range(4):
+                copy(step, 1, place, layer + 1, k).start()
+
+        @pl.when(below)
+        def _():
+            for k in range(4):
+                copy(step, 2, place, layer - 1, k).start()
+
+        for k in range(1, 4):
+            copy(step, 0, place, layer, k).start()
+
+    def receive(step):
+        for k in range(1, 4):
+            copy(step, 0, (place + 4 - k) % 4, layer, k).wait_recv()
+
+        @pl.when(below)
+        def _():
+            for k in range(4):
+                copy(step, 1, (place + 4 - k) % 4, layer - 1, k).wait_recv()
+
+        @pl.when(above)
+        def _():
+            for k in range(4):
+                copy(step, 2, (place + 4 - k) % 4, layer + 1, k).wait_recv()
+
+    def finish(step):
+        @pl.when(above)
+        def _():
+            for k in range(4):
+                copy(step, 1, place, layer + 1, k).wait_send()
+
+        @pl.when(below)
+        def _():
+            for k in range(4):
+                copy(step, 2, place, layer - 1, k).wait_send()
+
+        for k in range(1, 4):
+            copy(step, 0, place, layer, k).wait_send()
+
+    return wait_entry, send, receive, finish
 
 
 VMEM = pl.BlockSpec(memory_space=pltpu.VMEM)
 SMEM = pl.BlockSpec(memory_space=pltpu.SMEM)
-FACE = jax.ShapeDtypeStruct((5, 8, 128), jnp.float32)
-FACES = jax.ShapeDtypeStruct((10, 8, 128), jnp.float32)
 STATE = jax.ShapeDtypeStruct((EDGE, 19, 8, 128), jnp.float32)
-ROWS = pltpu.VMEM((5, EDGE, 128), jnp.float32)
-GHOSTS = pltpu.VMEM((5, EDGE + 8, 128), jnp.float32)
-LIMIT = pltpu.CompilerParams(vmem_limit_bytes=40 * 2**20)
-
-
-def exchange(xy, zu, zd):
-    layers = lax.axis_size("blocks") // 4
-    return pl.pallas_call(
-        functools.partial(exchange_kernel, layers),
-        out_shape=[
-            jax.ShapeDtypeStruct((4, 10, 8, 128), jnp.float32),
-            jax.ShapeDtypeStruct((4, 5, 8, 128), jnp.float32),
-            jax.ShapeDtypeStruct((4, 5, 8, 128), jnp.float32),
-        ],
-        in_specs=[VMEM] * 3,
-        out_specs=[VMEM] * 3,
-        scratch_shapes=[pltpu.SemaphoreType.DMA((11,)), pltpu.SemaphoreType.DMA((11,))],
-        compiler_params=pltpu.CompilerParams(collective_id=0, has_side_effects=True),
-    )(xy, zu, zd)
 
 
 CHUNKS = ((0, 0, 10), (1, 0, 10), (0, 10, 19), (1, 10, 19))
@@ -581,9 +568,12 @@
         each(lambda d: hand(k, d, place).start())
         out[2 * place + plane, low:high] = sorted_[k][place]
 
-    for k in range(parts):
+    def begin(k):
         keep(k).start()
         each(lambda d: spread(k, d, place).start())
+
+    begin(0)
+    begin(1)
     for k in range(parts):
         keep(k).wait()
         each(lambda d: spread(k, d, peer(16 - d)).wait_recv())
@@ -594,6 +584,8 @@
 
         lax.fori_loop(0, room, pick, 0)
         swap(k).start()
+        if k + 2 < parts:
+            begin(k + 2)
         if k > 0:
             deliver(k - 1)
     deliver(parts - 1)
@@ -659,7 +651,7 @@
         out_shape=jax.ShapeDtypeStruct((EDGE, slots * 152, 128), jnp.float32),
         in_specs=[pl.BlockSpec((slots, 19, planes * 1024), lambda g: (0, 0, g))],
         out_specs=pl.BlockSpec((planes, slots * 152, 128), lambda g: (g, 0, 0)),
-        compiler_params=LIMIT,
+        compiler_params=pltpu.CompilerParams(vmem_limit_bytes=58 * 2**20),
     )(old_pdfs)
     if peers == EDGE and slots == 2:
         plan, most = migration_plan(old_slot)
@@ -687,33 +679,30 @@
 def per_device(old_pdfs, old_slot, neighbours, cell_flags):
     state = migrate(old_pdfs, old_slot)
     flags = cell_flags.reshape(EDGE, 8, 128)
-    c, xy, zu, zd = pl.pallas_call(
-        first_kernel,
-        out_shape=[STATE, FACES, FACE, FACE],
-        in_specs=[SMEM, VMEM],
-        out_specs=[VMEM] * 4,
-        scratch_shapes=[ROWS],
-        compiler_params=LIMIT,
-    )(neighbours, state)
-    for _ in range(STEPS - 1):
-        rxy, rb, ra = exchange(xy, zu, zd)
-        c, xy, zu, zd = pl.pallas_call(
-            middle_kernel,
-            out_shape=[STATE, FACES, FACE, FACE],
-            in_specs=[SMEM] + [VMEM] * 5,
-            out_specs=[VMEM] * 4,
-            scratch_shapes=[ROWS, GHOSTS],
-            compiler_params=LIMIT,
-        )(neighbours, flags, c, rxy, rb, ra)
-    rxy, rb, ra = exchange(xy, zu, zd)
+    layers = lax.axis_size("blocks") // 4
+
+    def tiles(*lead):
+        return pltpu.VMEM(lead + (8, 128), jnp.float32)
+
     return pl.pallas_call(
-        last_kernel,
+        functools.partial(steps_kernel, layers),
         out_shape=jax.ShapeDtypeStruct((1, 19, EDGE * EDGE * EDGE), jnp.float32),
-        in_specs=[SMEM] + [VMEM] * 5,
+        in_specs=[SMEM, VMEM, VMEM],
         out_specs=VMEM,
-        scratch_shapes=[GHOSTS, pltpu.VMEM((152, 128), jnp.float32)],
-        compiler_params=LIMIT,
-    )(neighbours, flags, c, rxy, rb, ra)
+        scratch_shapes=[tiles(EDGE, 19)] * 2
+        + [tiles(10), tiles(5), tiles(5)] * STEPS
+        + [tiles(4, 10), tiles(4, 5), tiles(4, 5)] * STEPS
+        + [
+            pltpu.VMEM((5, EDGE, 128), jnp.float32),
+            pltpu.VMEM((5, EDGE + 8, 128), jnp.float32),
+            pltpu.VMEM((152, 128), jnp.float32),
+            pltpu.SemaphoreType.DMA((STEPS, 12)),
+            pltpu.SemaphoreType.DMA((STEPS, 12)),
+        ],
+        compiler_params=pltpu.CompilerParams(
+            collective_id=0, has_side_effects=True, vmem_limit_bytes=40 * 2**20
+        ),
+    )(neighbours, flags, state)
 
 
 def solution(mesh):

time: 199 us -> 186 us (0.935)
  local copies, waits for them, and re-layouts: 21.5 us -> 12.1 us
  Pallas kernels: 171 us -> 167 us
    pallas_call x5 -> x1, Pallas kernels: 39.5 us -> 29.8 us  [per_device(): pl.pallas_call(functools.partial(steps_kernel, layers), out_shape=jax.Sha...]
    unnamed x33 -> x5, local copies, waits for them, and re-layouts: 17.4 us -> 7.98 us
    pallas_call x1, Pallas kernels: 1.78 us -> 7.82 us  [migrate(): pl.pallas_call(functools.partial(spread_kernel, planes, slots), grid=(EDG...]
where the time goes in v3:
time: 186 us; the launch traced here: 183 us
  Pallas kernels  167 us (90%)
  local copies, waits for them, and re-layouts  12.1 us (7%)
  other arithmetic  3.06 us (2%)
    pallas_call x1, Pallas kernels, migrate_with(): pl.pallas_call(functools.partial(migrate_kernel, room), out_shape=STATE,...  129 us
    pallas_call x1, Pallas kernels, per_device(): pl.pallas_call(functools.partial(steps_kernel, layers), out_shape=jax.Sha...  29.8 us
    unnamed x5, local copies, waits for them, and re-layouts  7.98 us
    pallas_call x1, Pallas kernels, migrate(): pl.pallas_call(functools.partial(spread_kernel, planes, slots), grid=(EDG...  7.82 us
    pallas_call x1, local copies, waits for them, and re-layouts, per_device(): pl.pallas_call(functools.partial(steps_kernel, layers), out_shape=jax.Sha...  4.01 us

profile of v3, /device:TPU:0, one launch (start us, length us, event | category | flops | bytes accessed | tf_op | source)
XLA Modules:
  0.0 183.5 jit_solution(16099459034388452614)
XLA Ops:
  0.0 0.7 fusion.7
  0.7 0.7 and_select_fusion
  1.3 0.7 compare_and_fusion
  2.0 0.2 convert_reduce_fusion
  2.2 0.1 select_reduce_fusion
  2.3 0.7 fusion.4
  4.4 0.1 constant_dynamic-slice_fusion
  4.5 8.0 %copy.7.old = f32[2,19,32768]{2,1,0:T(8,128)} copy(f32[2,19,32768]{2,0,1:T(2,128)} %param.7) | data formatting | bytes 9961472 | tf_op args[0]
  12.5 7.8 %shard_map.46 = f32[32,304,128]{2,1,0:T(8,128)} custom-call(f32[2,19,32768]{2,1,0:T(8,128)} %copy.7.old), custom_call_target="tpu_custom_call" | custom-call | tf_op jit(solution)/shard_map/pallas_call | solution.py:648
  20.3 0.0 copy-start
  20.3 0.0 copy-start.1
  20.3 129.3 %conditional.1 = (f32[32,19,8,128]{3,2,1,0:T(8,128)S(1)}) conditional(s32[]{:T(128)} %clamp.3, (s32[4,16]{1,0:T(4,128)S(1)}, f32[32,2,19,8,128]{4,3,2,1,0:T(8,128)}) %tuple.23, (s32[4,16]{1,0:T(4,128)S(1)}, f32[32,2,19,8,128]{4,3,2,1,0:T(8,128)}) %tuple.24, (s32[4,16]{1,0:T(4,128)S(1)}, f32[32,2,19,8,128]{4,3,2,1,0:T(8,128)}) %tuple.25), branch_computations={%region_4.5_spmd, %region_5.6_spmd, %region_6.7_spmd} | conditional | bytes 8 | solution.py:664
  20.3 129.3 %branch_0_fun.1 = f32[32,19,8,128]{3,2,1,0:T(8,128)S(1)} custom-call(s32[4,16]{1,0:T(4,128)S(1)} %get-tuple-element.20.plan, f32[32,2,19,8,128]{4,3,2,1,0:T(8,128)} %get-tuple-element.22.tiles), custom_call_target="tpu_custom_call" | custom-call | tf_op jit(solution)/shard_map/cond/branch_0_fun/pallas_call | solution.py:607
  149.6 0.0 copy-done
  149.7 0.0 copy-done.1
  149.7 29.8 %shard_map.47 = f32[1,19,32768]{2,1,0:T(8,128)S(1)} custom-call(s32[1,18]{1,0:T(1,128)S(1)} %copy-done.1, s32[32,8,128]{2,1,0:T(8,128)S(1)} %bitcast.8, f32[32,19,8,128]{3,2,1,0:T(8,128)S(1)} %get-tuple-element.35.f), custom_call_target="tpu_custom_call" | custom-call | tf_op jit(solution)/shard_map/pallas_call | solution.py:687
  179.5 4.0 %copy.8 = f32[1,19,32768]{2,0,1:T(1,128)} copy(f32[1,19,32768]{2,1,0:T(8,128)S(1)} %shard_map.47) | data formatting | bytes 4980736 | tf_op jit(solution)/shard_map/pallas_call | solution.py:687
  (5 shorter events, 0.0 us)
Async XLA Ops:
  20.3 129.3 %copy-start = (s32[1,32768]{1,0:T(1,128)S(1)}, s32[1,32768]{1,0:T(1,128)}, u32[]{:S(2)}) copy-start(s32[1,32768]{1,0:T(1,128)} %param.10) | copy-start | bytes 393220
  20.3 129.4 %copy-start.1 = (s32[1,18]{1,0:T(1,128)S(1)}, s32[1,18]{1,0:T(1,128)}, u32[]{:S(2)}) copy-start(s32[1,18]{1,0:T(1,128)} %nbr.1) | copy-start | bytes 220

commit v4 on v3

--- a/solution.py
+++ b/solution.py
@@ -338,7 +338,7 @@
 
 def steps_kernel(layers, nbr, flags, f, out, *scratch):
     c, messages, landed = scratch[:2], scratch[2 : 2 + 3 * STEPS], scratch[2 + 3 * STEPS : 2 + 6 * STEPS]
-    rows, gy, lines, send_sem, recv_sem = scratch[2 + 6 * STEPS :]
+    rows, gy, send_sem, recv_sem = scratch[2 + 6 * STEPS :]
     wait_entry, send, receive, finish = exchanges(layers, messages, landed, send_sem, recv_sem)
     for step in range(STEPS):
         now, before = c[step % 2], c[(step + 1) % 2]
@@ -372,10 +372,7 @@
     def last_plane(x, carry):
         new = pull(x, nbr, now, rxy, rb, ra, flags, gy)
         for i in range(19):
-            lines[8 * i : 8 * i + 8, :] = new[i]
-        for s in range(8):
-            at = pl.multiple_of(x * 1024 + s * 128, 128)
-            out[0, :, pl.ds(at, 128)] = lines[pl.ds(s, 19, stride=8), :]
+            out[i, x] = new[i]
         return carry
 
     lax.fori_loop(0, EDGE, last_plane, 0)
@@ -486,7 +483,7 @@
 CAPACITIES = (10, 12, 16)
 
 
-def migrate_kernel(room, plan, tiles, out, *scratch):
+def migrate_kernel(room, plan, old, out, *scratch):
     parts = len(CHUNKS)
     held, wanted, given, sorted_ = (scratch[parts * n : parts * n + parts] for n in range(4))
     own_sem, send_one, recv_one, send_two, recv_two, send_three, recv_three = scratch[4 * parts :]
@@ -513,8 +510,8 @@
     def spread(k, d, owner):
         plane, low, high = CHUNKS[k]
         return pltpu.make_async_remote_copy(
-            src_ref=tiles.at[2 * peer(d) + plane, :, low:high],
-            dst_ref=held[k].at[pl.ds(2 * owner, 2)],
+            src_ref=old.at[low:high, pl.ds(pl.multiple_of(32 * peer(d) + 16 * plane, 16), 16)],
+            dst_ref=held[k].at[owner],
             send_sem=send_one.at[k, d],
             recv_sem=recv_one.at[k, d],
             device_id=device(d),
@@ -524,7 +521,9 @@
     def keep(k):
         plane, low, high = CHUNKS[k]
         return pltpu.make_async_copy(
-            tiles.at[2 * place + plane, :, low:high], held[k].at[pl.ds(2 * place, 2)], own_sem.at[k]
+            old.at[low:high, pl.ds(pl.multiple_of(32 * place + 16 * plane, 16), 16)],
+            held[k].at[place],
+            own_sem.at[k],
         )
 
     def swap(k):
@@ -555,12 +554,17 @@
 
         lax.fori_loop(1, 16, step, 0)
 
+    def slot_of(k, slot):
+        first = held[k][slot // 2, :, pl.ds(0, 8, stride=2), :]
+        second = held[k][slot // 2, :, pl.ds(1, 8, stride=2), :]
+        return jnp.where(slot % 2 > 0, second, first)
+
     def deliver(k):
         plane, low, high = CHUNKS[k]
         swap(k).wait_recv()
 
         def choose(b, carry):
-            near, far = held[k][plan[2, b]], given[k][plan[3, b]]
+            near, far = slot_of(k, plan[2, b]), given[k][plan[3, b]]
             sorted_[k][b] = jnp.where(plan[1, b] > 0, near, far)
             return carry
 
@@ -579,7 +583,7 @@
         each(lambda d: spread(k, d, peer(16 - d)).wait_recv())
 
         def pick(e, carry):
-            wanted[k][e] = held[k][plan[0, e]]
+            wanted[k][e] = slot_of(k, plan[0, e])
             return carry
 
         lax.fori_loop(0, room, pick, 0)
@@ -597,19 +601,19 @@
         each(lambda d: hand(k, d, place).wait_send())
 
 
-def migrate_with(room, number, plan, tiles):
+def migrate_with(room, number, plan, old):
     parts = len(CHUNKS)
 
-    def buffers(count):
-        return [pltpu.VMEM((count, high - low, 8, 128), jnp.float32) for _, low, high in CHUNKS]
+    def buffers(count, rows=8):
+        return [pltpu.VMEM((count, high - low, rows, 128), jnp.float32) for _, low, high in CHUNKS]
 
     dma = pltpu.SemaphoreType.DMA
     return pl.pallas_call(
         functools.partial(migrate_kernel, room),
         out_shape=STATE,
-        in_specs=[SMEM, VMEM],
+        in_specs=[SMEM, pl.BlockSpec(memory_space=pl.ANY)],
         out_specs=VMEM,
-        scratch_shapes=buffers(32)
+        scratch_shapes=buffers(16, 16)
         + buffers(room)
         + buffers(room)
         + buffers(16)
@@ -618,32 +622,58 @@
         compiler_params=pltpu.CompilerParams(
             collective_id=number, has_side_effects=True, vmem_limit_bytes=40 * 2**20
         ),
-    )(plan, tiles)
-
-
-def migration_plan(old_slot):
+    )(plan, old)
+
+
+def plan_kernel(old_slot, plan, branch):
     half = lax.axis_index("blocks") // 16
-    block = jnp.arange(32, dtype=jnp.int32)
-    from_half, to_half = old_slot // 32, block // 16
-    crosses = from_half != to_half
-    same = (to_half[None, :] == to_half[:, None]) & (block[None, :] < block[:, None])
-    rank = jnp.sum((same & crosses[None, :]).astype(jnp.int32), axis=1)
-    leaves = crosses & (from_half == half)
-    entry = jnp.arange(16, dtype=jnp.int32)
-    chosen = leaves[None, :] & (rank[None, :] == entry[:, None])
-    local = old_slot % 32
-    wanted = jnp.sum(jnp.where(chosen, local[None, :], 0), axis=1)
-    mine = lax.dynamic_slice_in_dim(jnp.stack([1 - crosses.astype(jnp.int32), local, rank]), half * 16, 16, 1)
-    stays = mine[0]
-    plan = jnp.stack([wanted, stays, mine[1] * stays, mine[2] * (1 - stays)])
-    counts = [jnp.sum((crosses & (to_half == h)).astype(jnp.int32)) for h in range(2)]
-    return plan, jnp.maximum(counts[0], counts[1])
+    for e in range(16):
+        plan[0, e] = 0
+
+    def block(b, counts):
+        slot = old_slot[b]
+        source, target = slot >> 5, b >> 4
+        crosses = (source != target).astype(jnp.int32)
+        rank = jnp.where(target == 0, counts[0], counts[1])
+
+        @pl.when(target == half)
+        def _():
+            plan[1, b & 15] = 1 - crosses
+            plan[2, b & 15] = (slot & 31) * (1 - crosses)
+            plan[3, b & 15] = rank * crosses
+
+        @pl.when((source == half) & (target != half))
+        def _():
+            plan[0, rank] = slot & 31
+
+        low = jnp.where(target == 0, crosses, 0)
+        return counts[0] + low, counts[1] + crosses - low
+
+    counts = lax.fori_loop(0, 32, block, (jnp.int32(0), jnp.int32(0)))
+    most = jnp.maximum(counts[0], counts[1])
+    branch[0] = sum((most > room).astype(jnp.int32) for room in CAPACITIES[:-1])
 
 
 def migrate(old_pdfs, old_slot):
     peers = lax.axis_size("blocks")
     slots = old_pdfs.shape[0]
     blocks = old_slot.shape[0]
+    if peers == EDGE and slots == 2:
+        plan, branch = pl.pallas_call(
+            plan_kernel,
+            out_shape=[
+                jax.ShapeDtypeStruct((4, 16), jnp.int32),
+                jax.ShapeDtypeStruct((1,), jnp.int32),
+            ],
+            in_specs=[SMEM],
+            out_specs=[SMEM, SMEM],
+        )(old_slot)
+        old = old_pdfs.reshape(slots, 19, 256, 128).transpose(1, 2, 0, 3).reshape(19, 512, 128)
+        calls = [
+            functools.partial(migrate_with, room, 1 + number)
+            for number, room in enumerate(CAPACITIES)
+        ]
+        return lax.switch(branch[0], calls, plan, old)
     planes = 4
     tiles = pl.pallas_call(
         functools.partial(spread_kernel, planes, slots),
@@ -653,15 +683,6 @@
         out_specs=pl.BlockSpec((planes, slots * 152, 128), lambda g: (g, 0, 0)),
         compiler_params=pltpu.CompilerParams(vmem_limit_bytes=58 * 2**20),
     )(old_pdfs)
-    if peers == EDGE and slots == 2:
-        plan, most = migration_plan(old_slot)
-        branch = sum((most > room).astype(jnp.int32) for room in CAPACITIES[:-1])
-        tiles = tiles.reshape(EDGE, slots, 19, 8, 128)
-        calls = [
-            functools.partial(migrate_with, room, 1 + number)
-            for number, room in enumerate(CAPACITIES)
-        ]
-        return lax.switch(branch, calls, plan, tiles)
     parts = peers // EDGE
     rows = 8 // parts
     if parts > 1:
@@ -684,9 +705,9 @@
     def tiles(*lead):
         return pltpu.VMEM(lead + (8, 128), jnp.float32)
 
-    return pl.pallas_call(
+    out = pl.pallas_call(
         functools.partial(steps_kernel, layers),
-        out_shape=jax.ShapeDtypeStruct((1, 19, EDGE * EDGE * EDGE), jnp.float32),
+        out_shape=jax.ShapeDtypeStruct((19, EDGE, 8, 128), jnp.float32),
         in_specs=[SMEM, VMEM, VMEM],
         out_specs=VMEM,
         scratch_shapes=[tiles(EDGE, 19)] * 2
@@ -695,7 +716,6 @@
         + [
             pltpu.VMEM((5, EDGE, 128), jnp.float32),
             pltpu.VMEM((5, EDGE + 8, 128), jnp.float32),
-            pltpu.VMEM((152, 128), jnp.float32),
             pltpu.SemaphoreType.DMA((STEPS, 12)),
             pltpu.SemaphoreType.DMA((STEPS, 12)),
         ],
@@ -703,6 +723,7 @@
             collective_id=0, has_side_effects=True, vmem_limit_bytes=40 * 2**20
         ),
     )(neighbours, flags, state)
+    return out.reshape(1, 19, EDGE * EDGE * EDGE)
 
 
 def solution(mesh):

time: 186 us -> 164 us (0.88)
  local copies, waits for them, and re-layouts: 12.1 us -> 1.46 us
  Pallas kernels: 167 us -> 159 us
  other arithmetic: 3.06 us -> 0 us
    unnamed x5, local copies, waits for them, and re-layouts: 7.98 us -> 1.46 us
    pallas_call x1, Pallas kernels: 7.82 us -> 1.76 us  [migrate(): pl.pallas_call(plan_kernel, out_shape=[jax.ShapeDtypeStruct((4, 16), jnp....]
    pallas_call x1 -> x0, local copies, waits for them, and re-layouts: 4.01 us -> none  [per_device(): pl.pallas_call(functools.partial(steps_kernel, layers), out_shape=jax.Sha...]
where the time goes in v4:
time: 164 us; the launch traced here: 161 us
  Pallas kernels  159 us (97%)
    pallas_call x1, Pallas kernels, migrate_with(): pl.pallas_call(functools.partial(migrate_kernel, room), out_shape=STATE,...  128 us
    pallas_call x1, Pallas kernels, per_device(): pl.pallas_call(functools.partial(steps_kernel, layers), out_shape=jax.Sha...  29.5 us

profile of v4, /device:TPU:0, one launch (start us, length us, event | category | flops | bytes accessed | tf_op | source)
XLA Modules:
  0.0 160.9 jit_solution(12175859270346247569)
XLA Ops:
  0.0 1.8 %shard_map.46 = (s32[4,16]{1,0:T(4,128)S(1)}, s32[1]{0:T(128)}) custom-call(s32[32]{0:T(128)} %old_slot.1), custom_call_target="tpu_custom_call" | custom-call | tf_op jit(solution)/shard_map/pallas_call | solution.py:662
  2.4 0.0 copy-start
  2.4 0.0 copy-start.1
  2.4 127.5 %conditional.1 = (f32[32,19,8,128]{3,2,1,0:T(8,128)S(1)}) conditional(s32[]{:T(128)} %bitcast.1, (s32[4,16]{1,0:T(4,128)S(1)}, f32[19,512,128]{2,1,0:T(8,128)}) %tuple.18, (s32[4,16]{1,0:T(4,128)S(1)}, f32[19,512,128]{2,1,0:T(8,128)}) %tuple.19, (s32[4,16]{1,0:T(4,128)S(1)}, f32[19,512,128]{2,1,0:T(8,128)}) %tuple.20), branch_computations={%region_0.0_spmd, %region_1.0_spmd, %region_2.0_spmd} | conditional | bytes 8 | solution.py:676
  2.5 127.5 %branch_0_fun.1 = f32[32,19,8,128]{3,2,1,0:T(8,128)S(1)} custom-call(s32[4,16]{1,0:T(4,128)S(1)} %get-tuple-element.20.plan, f32[19,512,128]{2,1,0:T(8,128)} %get-tuple-element.22.old), custom_call_target="tpu_custom_call" | custom-call | tf_op jit(solution)/shard_map/cond/branch_0_fun/pallas_call | solution.py:611
  130.0 0.0 copy-done
  130.0 0.0 copy-done.1
  130.0 29.5 %shard_map.47 = f32[19,32,8,128]{3,2,1,0:T(8,128)S(1)} custom-call(s32[1,18]{1,0:T(1,128)S(1)} %copy-done.1, s32[32,8,128]{2,1,0:T(8,128)S(1)} %bitcast.9, f32[32,19,8,128]{3,2,1,0:T(8,128)S(1)} %get-tuple-element.31.f), custom_call_target="tpu_custom_call" | custom-call | tf_op jit(solution)/shard_map/pallas_call | solution.py:708
  159.5 1.5 copy.13
Async XLA Ops:
  2.4 127.6 %copy-start = (s32[1,32768]{1,0:T(1,128)S(1)}, s32[1,32768]{1,0:T(1,128)}, u32[]{:S(2)}) copy-start(s32[1,32768]{1,0:T(1,128)} %param.10) | copy-start | bytes 393220
  2.4 127.6 %copy-start.1 = (s32[1,18]{1,0:T(1,128)S(1)}, s32[1,18]{1,0:T(1,128)}, u32[]{:S(2)}) copy-start(s32[1,18]{1,0:T(1,128)} %nbr.1) | copy-start | bytes 220

commit v5 on v4

--- a/solution.py
+++ b/solution.py
@@ -479,38 +479,60 @@
 STATE = jax.ShapeDtypeStruct((EDGE, 19, 8, 128), jnp.float32)
 
 
-CHUNKS = ((0, 0, 10), (1, 0, 10), (0, 10, 19), (1, 10, 19))
-CAPACITIES = (10, 12, 16)
-
-
-def migrate_kernel(room, plan, old, out, *scratch):
+CHUNKS = tuple((plane, low, high) for low, high in ((0, 10), (10, 19)) for plane in range(4))
+CAPACITIES = (9, 10, 12, 16)
+AHEAD = 3
+
+
+def migrate_kernel(room, levels, plan, old, out, *scratch):
     parts = len(CHUNKS)
-    held, wanted, given, sorted_ = (scratch[parts * n : parts * n + parts] for n in range(4))
-    own_sem, send_one, recv_one, send_two, recv_two, send_three, recv_three = scratch[4 * parts :]
+    held, up_out, up_in, down_out, down_in, sorted_ = (
+        scratch[parts * n : parts * n + parts] for n in range(6)
+    )
+    sems = scratch[6 * parts :]
+    own_sem, send_up, recv_up, send_down, recv_down = sems[:5]
+    send_one, recv_one, send_three, recv_three = sems[5:]
     me = lax.axis_index("blocks")
-    half, place = me // 16, me % 16
-    partner = (1 - half) * 16 + place
+    level, place = me // 8, me % 8
+    above, below = level + 1 < levels, level > 0
 
     def peer(d):
-        return (place + d) % 16
+        return (place + d) % 8
 
     def device(d):
-        return (half * 16 + peer(d),)
+        return (level * 8 + peer(d),)
 
     barrier = pltpu.get_barrier_semaphore()
 
-    def greet(d, carry):
-        pl.semaphore_signal(barrier, inc=1, device_id=device(d), device_id_type=MESH)
-        return carry
-
-    lax.fori_loop(1, 16, greet, 0)
-    pl.semaphore_signal(barrier, inc=1, device_id=(partner,), device_id_type=MESH)
-    pl.semaphore_wait(barrier, 16)
+    def greet(target):
+        pl.semaphore_signal(barrier, inc=1, device_id=target, device_id_type=MESH)
+
+    def each(body):
+        def step(d, carry):
+            body(d)
+            return carry
+
+        lax.fori_loop(1, 8, step, 0)
+
+    each(lambda d: greet(device(d)))
+
+    @pl.when(above)
+    def _():
+        greet((me + 8,))
+
+    @pl.when(below)
+    def _():
+        greet((me - 8,))
+
+    pl.semaphore_wait(barrier, 7 + above.astype(jnp.int32) + below.astype(jnp.int32))
+
+    def piece(k, owner):
+        plane, low, high = CHUNKS[k]
+        return old.at[low:high, pl.ds(pl.multiple_of(64 * owner + 16 * plane, 16), 16)]
 
     def spread(k, d, owner):
-        plane, low, high = CHUNKS[k]
         return pltpu.make_async_remote_copy(
-            src_ref=old.at[low:high, pl.ds(pl.multiple_of(32 * peer(d) + 16 * plane, 16), 16)],
+            src_ref=piece(k, peer(d)),
             dst_ref=held[k].at[owner],
             send_sem=send_one.at[k, d],
             recv_sem=recv_one.at[k, d],
@@ -519,20 +541,25 @@
         )
 
     def keep(k):
-        plane, low, high = CHUNKS[k]
-        return pltpu.make_async_copy(
-            old.at[low:high, pl.ds(pl.multiple_of(32 * place + 16 * plane, 16), 16)],
-            held[k].at[place],
-            own_sem.at[k],
-        )
-
-    def swap(k):
+        return pltpu.make_async_copy(piece(k, place), held[k].at[place], own_sem.at[k])
+
+    def rise(k, target):
         return pltpu.make_async_remote_copy(
-            src_ref=wanted[k],
-            dst_ref=given[k],
-            send_sem=send_two.at[k],
-            recv_sem=recv_two.at[k],
-            device_id=(partner,),
+            src_ref=up_out[k],
+            dst_ref=up_in[k],
+            send_sem=send_up.at[k],
+            recv_sem=recv_up.at[k],
+            device_id=(target,),
+            device_id_type=MESH,
+        )
+
+    def sink(k, target):
+        return pltpu.make_async_remote_copy(
+            src_ref=down_out[k],
+            dst_ref=down_in[k],
+            send_sem=send_down.at[k],
+            recv_sem=recv_down.at[k],
+            device_id=(target,),
             device_id_type=MESH,
         )
 
@@ -540,65 +567,101 @@
         plane, low, high = CHUNKS[k]
         return pltpu.make_async_remote_copy(
             src_ref=sorted_[k].at[peer(d)],
-            dst_ref=out.at[2 * owner + plane, low:high],
+            dst_ref=out.at[4 * owner + plane, low:high],
             send_sem=send_three.at[k, d],
             recv_sem=recv_three.at[k, d],
             device_id=device(d),
             device_id_type=MESH,
         )
 
-    def each(body):
-        def step(d, carry):
-            body(d)
-            return carry
-
-        lax.fori_loop(1, 16, step, 0)
-
     def slot_of(k, slot):
         first = held[k][slot // 2, :, pl.ds(0, 8, stride=2), :]
         second = held[k][slot // 2, :, pl.ds(1, 8, stride=2), :]
         return jnp.where(slot % 2 > 0, second, first)
 
+    def go_up(k, wait):
+        if wait:
+            rise(k, me - 8).wait_recv()
+
+        def pick(e, carry):
+            new = slot_of(k, plan[1, e])
+            up_out[k][e] = jnp.where(plan[0, e] > 0, up_in[k][plan[2, e]], new) if wait else new
+            return carry
+
+        lax.fori_loop(0, room, pick, 0)
+        rise(k, me + 8).start()
+
+    def go_down(k, wait):
+        if wait:
+            sink(k, me + 8).wait_recv()
+
+        def pick(e, carry):
+            new = slot_of(k, plan[4, e])
+            down_out[k][e] = jnp.where(plan[3, e] > 0, down_in[k][plan[5, e]], new) if wait else new
+            return carry
+
+        lax.fori_loop(0, room, pick, 0)
+        sink(k, me - 8).start()
+
     def deliver(k):
         plane, low, high = CHUNKS[k]
-        swap(k).wait_recv()
+
+        @pl.when(level == levels - 1)
+        def _():
+            rise(k, me - 8).wait_recv()
+
+        @pl.when(level == 0)
+        def _():
+            sink(k, me + 8).wait_recv()
 
         def choose(b, carry):
-            near, far = slot_of(k, plan[2, b]), given[k][plan[3, b]]
-            sorted_[k][b] = jnp.where(plan[1, b] > 0, near, far)
+            kind = plan[6, b]
+            value = jnp.where(kind == 1, up_in[k][plan[8, b]], down_in[k][plan[8, b]])
+            sorted_[k][b] = jnp.where(kind == 0, slot_of(k, plan[7, b]), value)
             return carry
 
-        lax.fori_loop(0, 16, choose, 0)
+        lax.fori_loop(0, 8, choose, 0)
         each(lambda d: hand(k, d, place).start())
-        out[2 * place + plane, low:high] = sorted_[k][place]
+        out[4 * place + plane, low:high] = sorted_[k][place]
 
     def begin(k):
         keep(k).start()
         each(lambda d: spread(k, d, place).start())
 
-    begin(0)
-    begin(1)
+    for k in range(AHEAD):
+        begin(k)
+    for turn in range(parts + levels - 1):
+        if turn < parts:
+            keep(turn).wait()
+            each(lambda d: spread(turn, d, peer(8 - d)).wait_recv())
+            if turn + AHEAD < parts:
+                begin(turn + AHEAD)
+        for lag in range(levels - 1):
+            if 0 <= turn - lag < parts:
+
+                @pl.when(level == lag)
+                def _():
+                    go_up(turn - lag, lag > 0)
+
+                @pl.when(level == levels - 1 - lag)
+                def _():
+                    go_down(turn - lag, lag > 0)
+
+        if turn >= levels - 1:
+            deliver(turn - levels + 1)
     for k in range(parts):
-        keep(k).wait()
-        each(lambda d: spread(k, d, peer(16 - d)).wait_recv())
-
-        def pick(e, carry):
-            wanted[k][e] = slot_of(k, plan[0, e])
-            return carry
-
-        lax.fori_loop(0, room, pick, 0)
-        swap(k).start()
-        if k + 2 < parts:
-            begin(k + 2)
-        if k > 0:
-            deliver(k - 1)
-    deliver(parts - 1)
-    for k in range(parts):
-        each(lambda d: hand(k, d, peer(16 - d)).wait_recv())
+        each(lambda d: hand(k, d, peer(8 - d)).wait_recv())
     for k in range(parts):
         each(lambda d: spread(k, d, place).wait_send())
-        swap(k).wait_send()
         each(lambda d: hand(k, d, place).wait_send())
+
+        @pl.when(above)
+        def _():
+            rise(k, me + 8).wait_send()
+
+        @pl.when(below)
+        def _():
+            sink(k, me - 8).wait_send()
 
 
 def migrate_with(room, number, plan, old):
@@ -609,48 +672,70 @@
 
     dma = pltpu.SemaphoreType.DMA
     return pl.pallas_call(
-        functools.partial(migrate_kernel, room),
+        functools.partial(migrate_kernel, room, lax.axis_size("blocks") // 8),
         out_shape=STATE,
         in_specs=[SMEM, pl.BlockSpec(memory_space=pl.ANY)],
         out_specs=VMEM,
-        scratch_shapes=buffers(16, 16)
-        + buffers(room)
-        + buffers(room)
-        + buffers(16)
-        + [dma((parts,)), dma((parts, 16)), dma((parts, 16)), dma((parts,)), dma((parts,))]
-        + [dma((parts, 16)), dma((parts, 16))],
+        scratch_shapes=buffers(8, 16)
+        + buffers(room) * 4
+        + buffers(8)
+        + [dma((parts,))] * 5
+        + [dma((parts, 8))] * 4,
         compiler_params=pltpu.CompilerParams(
-            collective_id=number, has_side_effects=True, vmem_limit_bytes=40 * 2**20
+            collective_id=number, has_side_effects=True, vmem_limit_bytes=48 * 2**20
         ),
     )(plan, old)
 
 
-def plan_kernel(old_slot, plan, branch):
-    half = lax.axis_index("blocks") // 16
-    for e in range(16):
-        plan[0, e] = 0
+def plan_kernel(levels, old_slot, plan, branch):
+    level = lax.axis_index("blocks") // 8
+    for row in range(9):
+        for e in range(16):
+            plan[row, e] = 0
+
+    def select(values, which):
+        return sum(jnp.where(which == n, value, 0) for n, value in enumerate(values))
 
     def block(b, counts):
+        ups, downs = counts
         slot = old_slot[b]
-        source, target = slot >> 5, b >> 4
-        crosses = (source != target).astype(jnp.int32)
-        rank = jnp.where(target == 0, counts[0], counts[1])
-
-        @pl.when(target == half)
-        def _():
-            plan[1, b & 15] = 1 - crosses
-            plan[2, b & 15] = (slot & 31) * (1 - crosses)
-            plan[3, b & 15] = rank * crosses
-
-        @pl.when((source == half) & (target != half))
-        def _():
-            plan[0, rank] = slot & 31
-
-        low = jnp.where(target == 0, crosses, 0)
-        return counts[0] + low, counts[1] + crosses - low
-
-    counts = lax.fori_loop(0, 32, block, (jnp.int32(0), jnp.int32(0)))
-    most = jnp.maximum(counts[0], counts[1])
+        source, target = slot // 16, b // 8
+        local = slot % 16
+
+        @pl.when((source <= level) & (target > level))
+        def _():
+            at = select(ups, level)
+            plan[0, at] = (source < level).astype(jnp.int32)
+            plan[1, at] = jnp.where(source == level, local, 0)
+            plan[2, at] = jnp.where(source < level, select(ups, level - 1), 0)
+
+        @pl.when((source >= level) & (target < level))
+        def _():
+            at = select(downs, level - 1)
+            plan[3, at] = (source > level).astype(jnp.int32)
+            plan[4, at] = jnp.where(source == level, local, 0)
+            plan[5, at] = jnp.where(source > level, select(downs, level), 0)
+
+        @pl.when(target == level)
+        def _():
+            at = b % 8
+            rank = jnp.where(source < level, select(ups, level - 1), select(downs, level))
+            plan[6, at] = jnp.where(source == level, 0, jnp.where(source < level, 1, 2))
+            plan[7, at] = jnp.where(source == level, local, 0)
+            plan[8, at] = jnp.where(source == level, 0, rank)
+
+        ups = tuple(
+            count + ((source <= n) & (target > n)).astype(jnp.int32) for n, count in enumerate(ups)
+        )
+        downs = tuple(
+            count + ((source > n) & (target <= n)).astype(jnp.int32)
+            for n, count in enumerate(downs)
+        )
+        return ups, downs
+
+    zeros = (jnp.int32(0),) * (levels - 1)
+    ups, downs = lax.fori_loop(0, 8 * levels, block, (zeros, zeros))
+    most = functools.reduce(jnp.maximum, ups + downs)
     branch[0] = sum((most > room).astype(jnp.int32) for room in CAPACITIES[:-1])
 
 
@@ -660,9 +745,9 @@
     blocks = old_slot.shape[0]
     if peers == EDGE and slots == 2:
         plan, branch = pl.pallas_call(
-            plan_kernel,
+            functools.partial(plan_kernel, peers // 8),
             out_shape=[
-                jax.ShapeDtypeStruct((4, 16), jnp.int32),
+                jax.ShapeDtypeStruct((9, 16), jnp.int32),
                 jax.ShapeDtypeStruct((1,), jnp.int32),
             ],
             in_specs=[SMEM],

time: 164 us -> 138 us (0.84); the launches traced: 161 us -> 138 us
  Pallas kernels: 159 us -> 136 us
    pallas_call x2, Pallas kernels: 129 us -> 108 us  [the longest x1 105 us: migrate_with(): pl.pallas_call(functools.partial(migrate_kernel, room, lax.axis_size('blo...]
where the time goes in v5:
time: 138 us
  Pallas kernels  136 us (99%)
  local copies, waits for them, and re-layouts  1.46 us (1%)
    pallas_call x1, Pallas kernels, migrate_with(): pl.pallas_call(functools.partial(migrate_kernel, room, lax.axis_size('blo...  105 us
    pallas_call x1, Pallas kernels, per_device(): pl.pallas_call(functools.partial(steps_kernel, layers), out_shape=jax.Sha...  27.9 us
    pallas_call x1, Pallas kernels, migrate(): pl.pallas_call(functools.partial(plan_kernel, peers // 8), out_shape=[jax...  3.13 us

profile of v5, /device:TPU:0, one launch (start us, length us, event | category | flops | bytes accessed | tf_op | source)
XLA Modules:
  0.0 137.7 jit_solution(10264520822161388109)
XLA Ops:
  0.0 3.1 %shard_map.46 = (s32[9,16]{1,0:T(8,128)S(1)}, s32[1]{0:T(128)}) custom-call(s32[32]{0:T(128)} %old_slot.1), custom_call_target="tpu_custom_call" | custom-call | tf_op jit(solution)/shard_map/pallas_call | solution.py:747
  3.8 0.0 copy-start
  3.8 0.0 copy-start.1
  3.8 104.5 %conditional.1 = (f32[32,19,8,128]{3,2,1,0:T(8,128)S(1)}) conditional(s32[]{:T(128)} %bitcast.1, (s32[9,16]{1,0:T(8,128)S(1)}, f32[19,512,128]{2,1,0:T(8,128)}) %tuple.22, (s32[9,16]{1,0:T(8,128)S(1)}, f32[19,512,128]{2,1,0:T(8,128)}) %tuple.23, (s32[9,16]{1,0:T(8,128)S(1)}, f32[19,512,128]{2,1,0:T(8,128)}) %tuple.24, ...), branch_computations={%region_0.0_spmd, %region_1.0_spmd, %region_2.0_spmd, %region_3.0_... | conditional | bytes 8 | solution.py:761
  3.8 104.5 %branch_0_fun.1 = f32[32,19,8,128]{3,2,1,0:T(8,128)S(1)} custom-call(s32[9,16]{1,0:T(8,128)S(1)} %get-tuple-element.24.plan, f32[19,512,128]{2,1,0:T(8,128)} %get-tuple-element.26.old), custom_call_target="tpu_custom_call" | custom-call | tf_op jit(solution)/shard_map/cond/branch_0_fun/pallas_call | solution.py:674
  108.4 0.0 copy-done
  108.4 0.0 copy-done.1
  108.4 27.9 %shard_map.47 = f32[19,32,8,128]{3,2,1,0:T(8,128)S(1)} custom-call(s32[1,18]{1,0:T(1,128)S(1)} %copy-done.1, s32[32,8,128]{2,1,0:T(8,128)S(1)} %bitcast.9, f32[32,19,8,128]{3,2,1,0:T(8,128)S(1)} %get-tuple-element.38.f), custom_call_target="tpu_custom_call" | custom-call | tf_op jit(solution)/shard_map/pallas_call | solution.py:793
  136.3 1.5 %copy.14 = f32[1,19,32768]{2,0,1:T(1,128)} copy(f32[1,19,32768]{2,0,1:T(1,128)S(1)} %bitcast.8) | data formatting | bytes 4980736
Async XLA Ops:
  3.8 104.6 %copy-start = (s32[1,32768]{1,0:T(1,128)S(1)}, s32[1,32768]{1,0:T(1,128)}, u32[]{:S(2)}) copy-start(s32[1,32768]{1,0:T(1,128)} %param.11) | copy-start | bytes 393220
  3.8 104.6 %copy-start.1 = (s32[1,18]{1,0:T(1,128)S(1)}, s32[1,18]{1,0:T(1,128)}, u32[]{:S(2)}) copy-start(s32[1,18]{1,0:T(1,128)} %nbr.1) | copy-start | bytes 220

commit v6 on v5

--- a/solution.py
+++ b/solution.py
@@ -360,7 +360,7 @@
             note_faces(x, nbr, collided, zu, zd, rows)
             return carry
 
-        lax.fori_loop(0, EDGE, plane, 0)
+        lax.fori_loop(0, EDGE, plane, 0, unroll=2)
         finish_faces(nbr, now, rows, xy)
         if step == 0:
             wait_entry()
@@ -375,7 +375,7 @@
             out[i, x] = new[i]
         return carry
 
-    lax.fori_loop(0, EDGE, last_plane, 0)
+    lax.fori_loop(0, EDGE, last_plane, 0, unroll=2)
     for step in range(STEPS):
         finish(step)
 
@@ -479,9 +479,9 @@
 STATE = jax.ShapeDtypeStruct((EDGE, 19, 8, 128), jnp.float32)
 
 
-CHUNKS = tuple((plane, low, high) for low, high in ((0, 10), (10, 19)) for plane in range(4))
+CHUNKS = tuple((plane, low, high) for low, high in ((0, 7), (7, 13), (13, 19)) for plane in range(4))
 CAPACITIES = (9, 10, 12, 16)
-AHEAD = 3
+AHEAD = 4
 
 
 def migrate_kernel(room, levels, plan, old, out, *scratch):
@@ -575,9 +575,9 @@
         )
 
     def slot_of(k, slot):
-        first = held[k][slot // 2, :, pl.ds(0, 8, stride=2), :]
-        second = held[k][slot // 2, :, pl.ds(1, 8, stride=2), :]
-        return jnp.where(slot % 2 > 0, second, first)
+        first = held[k][slot >> 1, :, pl.ds(0, 8, stride=2), :]
+        second = held[k][slot >> 1, :, pl.ds(1, 8, stride=2), :]
+        return jnp.where((slot & 1) > 0, second, first)
 
     def go_up(k, wait):
         if wait:
@@ -699,8 +699,8 @@
     def block(b, counts):
         ups, downs = counts
         slot = old_slot[b]
-        source, target = slot // 16, b // 8
-        local = slot % 16
+        source, target = slot >> 4, b >> 3
+        local = slot & 15
 
         @pl.when((source <= level) & (target > level))
         def _():
@@ -718,7 +718,7 @@
 
         @pl.when(target == level)
         def _():
-            at = b % 8
+            at = b & 7
             rank = jnp.where(source < level, select(ups, level - 1), select(downs, level))
             plan[6, at] = jnp.where(source == level, 0, jnp.where(source < level, 1, 2))
             plan[7, at] = jnp.where(source == level, local, 0)

time: 138 us -> 129 us (0.935)
  Pallas kernels: 136 us -> 127 us
    pallas_call x1, Pallas kernels: 27.9 us -> 22.6 us  [per_device(): pl.pallas_call(functools.partial(steps_kernel, layers), out_shape=jax.Sha...]
    pallas_call x1, Pallas kernels: 105 us -> 101 us  [migrate_with(): pl.pallas_call(functools.partial(migrate_kernel, room, lax.axis_size('blo...]
where the time goes in v6:
time: 129 us
  Pallas kernels  127 us (98%)
  local copies, waits for them, and re-layouts  1.46 us (1%)
    pallas_call x1, Pallas kernels, migrate_with(): pl.pallas_call(functools.partial(migrate_kernel, room, lax.axis_size('blo...  101 us
    pallas_call x1, Pallas kernels, per_device(): pl.pallas_call(functools.partial(steps_kernel, layers), out_shape=jax.Sha...  22.6 us
    pallas_call x1, Pallas kernels, migrate(): pl.pallas_call(functools.partial(plan_kernel, peers // 8), out_shape=[jax...  2.83 us

profile of v6, /device:TPU:0, one launch (start us, length us, event | category | flops | bytes accessed | tf_op | source)
XLA Modules:
  0.0 128.9 jit_solution(12050519539945015389)
XLA Ops:
  0.0 2.8 %shard_map.46 = (s32[9,16]{1,0:T(8,128)S(1)}, s32[1]{0:T(128)}) custom-call(s32[32]{0:T(128)} %old_slot.1), custom_call_target="tpu_custom_call" | custom-call | tf_op jit(solution)/shard_map/pallas_call | solution.py:747
  3.5 0.0 copy-start
  3.5 0.0 copy-start.1
  3.5 101.3 %conditional.1 = (f32[32,19,8,128]{3,2,1,0:T(8,128)S(1)}) conditional(s32[]{:T(128)} %bitcast.1, (s32[9,16]{1,0:T(8,128)S(1)}, f32[19,512,128]{2,1,0:T(8,128)}) %tuple.22, (s32[9,16]{1,0:T(8,128)S(1)}, f32[19,512,128]{2,1,0:T(8,128)}) %tuple.23, (s32[9,16]{1,0:T(8,128)S(1)}, f32[19,512,128]{2,1,0:T(8,128)}) %tuple.24, ...), branch_computations={%region_0.0_spmd, %region_1.0_spmd, %region_2.0_spmd, %region_3.0_... | conditional | bytes 8 | solution.py:761
  3.5 101.3 %branch_0_fun.1 = f32[32,19,8,128]{3,2,1,0:T(8,128)S(1)} custom-call(s32[9,16]{1,0:T(8,128)S(1)} %get-tuple-element.24.plan, f32[19,512,128]{2,1,0:T(8,128)} %get-tuple-element.26.old), custom_call_target="tpu_custom_call" | custom-call | tf_op jit(solution)/shard_map/cond/branch_0_fun/pallas_call | solution.py:674
  104.8 0.0 copy-done
  104.9 0.0 copy-done.1
  104.9 22.6 %shard_map.47 = f32[19,32,8,128]{3,2,1,0:T(8,128)S(1)} custom-call(s32[1,18]{1,0:T(1,128)S(1)} %copy-done.1, s32[32,8,128]{2,1,0:T(8,128)S(1)} %bitcast.9, f32[32,19,8,128]{3,2,1,0:T(8,128)S(1)} %get-tuple-element.38.f), custom_call_target="tpu_custom_call" | custom-call | tf_op jit(solution)/shard_map/pallas_call | solution.py:793
  127.4 1.5 %copy.14 = f32[1,19,32768]{2,0,1:T(1,128)} copy(f32[1,19,32768]{2,0,1:T(1,128)S(1)} %bitcast.8) | data formatting | bytes 4980736
Async XLA Ops:
  3.5 101.4 %copy-start = (s32[1,32768]{1,0:T(1,128)S(1)}, s32[1,32768]{1,0:T(1,128)}, u32[]{:S(2)}) copy-start(s32[1,32768]{1,0:T(1,128)} %param.11) | copy-start | bytes 393220
  3.5 101.4 %copy-start.1 = (s32[1,18]{1,0:T(1,128)S(1)}, s32[1,18]{1,0:T(1,128)}, u32[]{:S(2)}) copy-start(s32[1,18]{1,0:T(1,128)} %nbr.1) | copy-start | bytes 220

commit v7 on v6

--- a/solution.py
+++ b/solution.py
@@ -480,8 +480,8 @@
 
 
 CHUNKS = tuple((plane, low, high) for low, high in ((0, 7), (7, 13), (13, 19)) for plane in range(4))
-CAPACITIES = (9, 10, 12, 16)
-AHEAD = 4
+CAPACITIES = (9, 10, 11, 13, 16)
+AHEAD = 2
 
 
 def migrate_kernel(room, levels, plan, old, out, *scratch):

time: 129 us -> 134 us (1.039)
  Pallas kernels: 127 us -> 131 us
    pallas_call x1, Pallas kernels: 101 us -> 106 us  [migrate_with(): pl.pallas_call(functools.partial(migrate_kernel, room, lax.axis_size('blo...]
where the time goes in v7:
time: 134 us
  Pallas kernels  131 us (98%)
  local copies, waits for them, and re-layouts  1.46 us (1%)
    pallas_call x1, Pallas kernels, migrate_with(): pl.pallas_call(functools.partial(migrate_kernel, room, lax.axis_size('blo...  106 us
    pallas_call x1, Pallas kernels, per_device(): pl.pallas_call(functools.partial(steps_kernel, layers), out_shape=jax.Sha...  22.5 us
    pallas_call x1, Pallas kernels, migrate(): pl.pallas_call(functools.partial(plan_kernel, peers // 8), out_shape=[jax...  2.83 us

profile of v7, /device:TPU:0, one launch (start us, length us, event | category | flops | bytes accessed | tf_op | source)
XLA Modules:
  0.0 133.5 jit_solution(15389228104230875984)
XLA Ops:
  0.0 2.8 %shard_map.46 = (s32[9,16]{1,0:T(8,128)S(1)}, s32[1]{0:T(128)}) custom-call(s32[32]{0:T(128)} %old_slot.1), custom_call_target="tpu_custom_call" | custom-call | tf_op jit(solution)/shard_map/pallas_call | solution.py:747
  3.5 0.0 copy-start
  3.5 0.0 copy-start.1
  3.5 106.1 %conditional.1 = (f32[32,19,8,128]{3,2,1,0:T(8,128)S(1)}) conditional(s32[]{:T(128)} %bitcast.1, (s32[9,16]{1,0:T(8,128)S(1)}, f32[19,512,128]{2,1,0:T(8,128)}) %tuple.26, (s32[9,16]{1,0:T(8,128)S(1)}, f32[19,512,128]{2,1,0:T(8,128)}) %tuple.27, (s32[9,16]{1,0:T(8,128)S(1)}, f32[19,512,128]{2,1,0:T(8,128)}) %tuple.28, ...), branch_computations={%region_0.0_spmd, %region_1.0_spmd, %region_2.0_spmd, %region_3.0_... | conditional | bytes 8 | solution.py:761
  3.5 105.8 %branch_0_fun.1 = f32[32,19,8,128]{3,2,1,0:T(8,128)S(1)} custom-call(s32[9,16]{1,0:T(8,128)S(1)} %get-tuple-element.26.plan, f32[19,512,128]{2,1,0:T(8,128)} %get-tuple-element.30.old), custom_call_target="tpu_custom_call" | custom-call | tf_op jit(solution)/shard_map/cond/branch_0_fun/pallas_call | solution.py:674
  109.6 0.0 copy-done
  109.6 0.0 copy-done.1
  109.6 22.5 %shard_map.47 = f32[19,32,8,128]{3,2,1,0:T(8,128)S(1)} custom-call(s32[1,18]{1,0:T(1,128)S(1)} %copy-done.1, s32[32,8,128]{2,1,0:T(8,128)S(1)} %bitcast.9, f32[32,19,8,128]{3,2,1,0:T(8,128)S(1)} %get-tuple-element.45.f), custom_call_target="tpu_custom_call" | custom-call | tf_op jit(solution)/shard_map/pallas_call | solution.py:793
  132.1 1.5 %copy.15 = f32[1,19,32768]{2,0,1:T(1,128)} copy(f32[1,19,32768]{2,0,1:T(1,128)S(1)} %bitcast.8) | data formatting | bytes 4980736
Async XLA Ops:
  3.5 106.1 %copy-start = (s32[1,32768]{1,0:T(1,128)S(1)}, s32[1,32768]{1,0:T(1,128)}, u32[]{:S(2)}) copy-start(s32[1,32768]{1,0:T(1,128)} %param.12) | copy-start | bytes 393220
  3.5 106.1 %copy-start.1 = (s32[1,18]{1,0:T(1,128)S(1)}, s32[1,18]{1,0:T(1,128)}, u32[]{:S(2)}) copy-start(s32[1,18]{1,0:T(1,128)} %nbr.1) | copy-start | bytes 220
